TPU v7x, 256 devices: a whole 4x4x8 slice. The times are simulated.
256 devices in a mesh: fx: 16 (over z, core), fy: 8 (over y, x_lo), sz: 2 (over x_hi).
Axes of the slice: x: 4 (x_hi: 2, x_lo: 2; x = x_hi * 2 + x_lo), y: 4, z: 8, core: 2. Of those that a mesh axis runs over, the one named last changes fastest.
Arguments:
- populations: float32 [19, 64, 64, 512], P(None, 'fx', 'fy', 'sz'), as said below
- relaxation: float32 [64, 64, 512], P('fx', 'fy', 'sz'), may hold values from 1 to 1.8
- struct_velocity: float32 [3, 65536], P(None, ('fy', 'sz')), may hold values from -0.12 to 0.12
- iface_count: int32 [16, 8, 2, 16], P('fx', 'fy', 'sz'), may hold values from 0 to 32, as said below
- iface_cell: int32 [16, 8, 2, 16, 32], P('fx', 'fy', 'sz'), may hold values from 0 to 8191
- rbf_node: int32 [16, 8, 2, 16, 16, 32], P('fx', 'fy', 'sz'), may hold values from 0 to 4095
- rbf_weight: float32 [16, 8, 2, 16, 16, 32], P('fx', 'fy', 'sz'), may hold values from 0 to 0.25
- disp_prev: float32 [3, 65536], P(None, ('fy', 'sz')), may hold values from -6 to 6
- node_mass: float32 [65536], P(('fy', 'sz')), may hold values from 0.5 to 2
- connect: int32 [16, 16, 8, 512], P('fx', ('fy', 'sz')), may hold values from 0 to 4351
- modulus: float32 [16, 16, 512], P('fx', ('fy', 'sz')), may hold values from 0.5 to 5
- strain_basis: float32 [24, 24], replicated, may hold values from -1.25 to 1.25
Outputs:
- populations_out: float32 [19, 64, 64, 512], P(None, 'fx', 'fy', 'sz')
- solution: float32 [3, 65536], P(None, ('fy', 'sz'))
- residual: float32 [3, 65536], P(None, ('fy', 'sz'))
Inputs may be any that keep to these rules, and one draw needn't show every extreme that they name: `iface_count`: slots below the count are live. For some index of the first dimension, one subdomain gets 32 live slots from every block of it. `connect`: values below 256 name the last 256 nodes of the previous subdomain. All populations are positive.
All inputs are finite; a program needn't handle non-finite values.
Results may differ from a plain program's by a relative error of at most 0.0003.
Values sent between devices are 32-bit elements; how exact they have to be, the bound alone decides.
A program may use at most 128 MiB of HBM per device.

v0:
```python
import jax
import jax.numpy as jnp
from jax import lax
from jax.sharding import PartitionSpec as P

STEPS = 2
ITERS = 3
BND = 256


PRECISE = lax.Precision.HIGHEST
VELOCITY_TABLE = [
    (0, 0, 0),
    (1, 0, 0),
    (-1, 0, 0),
    (0, 1, 0),
    (0, -1, 0),
    (0, 0, 1),
    (0, 0, -1),
    (1, 1, 0),
    (-1, -1, 0),
    (1, -1, 0),
    (-1, 1, 0),
    (1, 0, 1),
    (-1, 0, -1),
    (1, 0, -1),
    (-1, 0, 1),
    (0, 1, 1),
    (0, -1, -1),
    (0, 1, -1),
    (0, -1, 1),
]
LATTICE_TABLE = [1.0 / 3.0] + [1.0 / 18.0] * 6 + [1.0 / 36.0] * 12
FORCE_SCALE = 20.0


def with_halo(x, sides, width):
    for axis, dim in sides:
        size, length = (lax.axis_size(axis), x.shape[dim])
        up = [(i, (i + 1) % size) for i in range(size)]
        down = [(j, i) for i, j in up]
        last = lax.slice_in_dim(x, length - width, length, axis=dim)
        initial = lax.slice_in_dim(x, 0, width, axis=dim)
        before = lax.ppermute(last, axis, up)
        after = lax.ppermute(initial, axis, down)
        x = jnp.concatenate([before, x, after], axis=dim)
    return x


def from_behind(value, axis, steps):
    count = lax.axis_size(axis)
    initial, last = (max(0, -steps), min(count, count - steps))
    return lax.ppermute(value, axis, [(source, source + steps) for source in range(initial, last)])


def moments(field, vel_table):
    density = jnp.sum(field, axis=0)
    momentum = jnp.einsum("iq,ixyz->qxyz", vel_table, field, precision=PRECISE)
    return (density, momentum)


def collide(field, relaxation, vel_table, lattice):
    density, momentum = moments(field, vel_table)
    flow_speed = momentum / density
    aligned = jnp.einsum("iq,qxyz->ixyz", vel_table, flow_speed, precision=PRECISE)
    square = jnp.sum(flow_speed * flow_speed, axis=0)
    balance = (
        lattice[:, None, None, None]
        * density
        * (1.0 + 3.0 * aligned + 4.5 * aligned * aligned - 1.5 * square)
    )
    return (field + relaxation * (balance - field), density)


def stream_whole(field):
    padded = with_halo(field, (("fx", 1), ("fy", 2), ("sz", 3)), 1)
    shape_x, shape_y, shape_z = (field.shape[1], field.shape[2], field.shape[3])
    shifted = []
    for corner in range(19):
        step_x, step_y, step_z = VELOCITY_TABLE[corner]
        shifted.append(
            padded[
                corner,
                1 - step_x : 1 - step_x + shape_x,
                1 - step_y : 1 - step_y + shape_y,
                1 - step_z : 1 - step_z + shape_z,
            ]
        )
    return jnp.stack(shifted)


def apply_operator(field, conn_local, mod_local, strain_basis, node_mass):
    node_count = field.shape[1]
    edge_rows = from_behind(field[:, node_count - BND :], ("fy", "sz"), 1)
    extended = jnp.concatenate([edge_rows, field], axis=1)
    picked = extended[:, conn_local].reshape(24, -1)
    strain = jnp.dot(strain_basis, picked, precision=PRECISE)
    spread = jnp.dot(strain_basis.T, strain, precision=PRECISE) * mod_local[None, :]
    spread = spread.reshape(3, -1)
    summed = jax.ops.segment_sum(spread.T, conn_local.reshape(-1), num_segments=BND + node_count).T
    summed = lax.psum(summed, "fx")
    returned = from_behind(summed[:, :BND], ("fy", "sz"), -1)
    result = node_mass[None, :] * field + summed[:, BND:]
    return result.at[:, node_count - BND :].add(returned)


def squares(vector):
    return lax.psum(jnp.sum(vector * vector), ("fy", "sz"))


def body(
    populations,
    relaxation,
    struct_velocity,
    iface_count,
    iface_cell,
    rbf_node,
    rbf_weight,
    disp_prev,
    node_mass,
    connect,
    modulus,
    strain_basis,
):
    vel_table = jnp.asarray(VELOCITY_TABLE, jnp.float32)
    lattice = jnp.asarray(LATTICE_TABLE, jnp.float32)
    owners = lax.axis_size(("fy", "sz"))
    node_count = disp_prev.shape[1]
    slot_count = iface_count.reshape(owners)
    slot_cells = iface_cell.reshape(owners, -1)
    slot_total = slot_cells.shape[1]
    support = rbf_node.reshape(owners, -1, slot_total)
    weights = rbf_weight.reshape(owners, -1, slot_total)
    live = (lax.broadcasted_iota(jnp.int32, (owners, slot_total), 1) < slot_count[:, None]).astype(
        jnp.float32
    )
    owner_base = lax.broadcasted_iota(jnp.int32, (owners, 1, 1), 0) * node_count
    whole_velocity = lax.all_gather(struct_velocity, ("fy", "sz"), axis=1, tiled=True)
    picked = whole_velocity[:, support + owner_base]
    wall = jnp.transpose(jnp.sum(weights * picked, axis=2), (1, 0, 2))
    wall_flat = jnp.transpose(wall, (1, 0, 2)).reshape(3, -1) * live.reshape(1, -1)
    live_flat = live.reshape(-1)
    flat_cells = slot_cells.reshape(-1)
    push = 6.0 * lattice[:, None] * jnp.dot(vel_table, wall_flat, precision=PRECISE)
    field = populations
    for section in range(STEPS):
        post, density = collide(field, relaxation, vel_table, lattice)
        at_cells = density.reshape(-1)[flat_cells]
        flat_post = post.reshape(19, -1).at[:, flat_cells].add(push * at_cells[None, :])
        post = flat_post.reshape(post.shape)
        field = stream_whole(post)
    density, momentum = moments(field, vel_table)
    rho_slot = density.reshape(-1)[flat_cells]
    mom_slot = momentum.reshape(3, -1)[:, flat_cells]
    force = (mom_slot - rho_slot[None, :] * wall_flat) * live_flat[None, :]
    force = jnp.transpose(force.reshape(3, owners, slot_total), (1, 2, 0))
    terms = weights[..., None] * force[:, None, :, :]
    partial_load = jax.ops.segment_sum(
        terms.reshape(-1, 3), (support + owner_base).reshape(-1), num_segments=owners * node_count
    ).T
    load = lax.psum_scatter(partial_load, ("fy", "sz"), scatter_dimension=1, tiled=True)
    load = lax.psum(load, "fx") * FORCE_SCALE
    conn_local = connect.reshape(8, -1)
    mod_local = modulus.reshape(-1)
    rhs = node_mass[None, :] * disp_prev + load
    solution = disp_prev
    residual = rhs - apply_operator(solution, conn_local, mod_local, strain_basis, node_mass)
    direction = residual
    norm_now = squares(residual)
    for section in range(ITERS):
        image = apply_operator(direction, conn_local, mod_local, strain_basis, node_mass)
        alpha = norm_now / lax.psum(jnp.sum(direction * image), ("fy", "sz"))
        solution = solution + alpha * direction
        residual = residual - alpha * image
        norm_next = squares(residual)
        direction = residual + norm_next / norm_now * direction
        norm_now = norm_next
    return (field, solution, residual)


def solution(mesh):
    return jax.shard_map(
        body,
        mesh=mesh,
        in_specs=(
            P(None, "fx", "fy", "sz"),
            P("fx", "fy", "sz"),
            P(None, ("fy", "sz")),
            P("fx", "fy", "sz", None),
            P("fx", "fy", "sz", None, None),
            P("fx", "fy", "sz", None, None, None),
            P("fx", "fy", "sz", None, None, None),
            P(None, ("fy", "sz")),
            P(("fy", "sz")),
            P("fx", ("fy", "sz"), None, None),
            P("fx", ("fy", "sz"), None),
            P(),
        ),
        out_specs=(P(None, "fx", "fy", "sz"), P(None, ("fy", "sz")), P(None, ("fy", "sz"))),
        check_vma=False,
    )
```

profile of v0, /device:TPU:1, one launch (start us, length us, event | category | flops | bytes accessed | tf_op | source)
XLA Modules:
  0.0 2271.4 jit_solution(4407093522506389737)
XLA Ops:
  11.8 697.2 %all_gather.3 = f32[3,65536]{0,1:T(8,128)} all-gather(f32[3,4096]{0,1:T(8,128)S(1)} %copy.316), channel_id=1, replica_groups=mesh['fx'=16,'fy'=8,'sz'=2] {'fy','sz'}, dimensions={1}, use_global_device_ids=true | all-gather | bytes 835584 | tf_op jit(solution)/shard_map/all_gather | solution.py:138
  712.3 38.3 %gather_fusion = f32[8192,3]{1,0:T(8,128)} fusion(f32[3,65536]{0,1:T(8,128)} %all_gather.3, s32[8192]{0:T(1024)S(1)} %broadcast_clamp_fusion), kind=kCustom, calls=%fused_computation | custom fusion | bytes 229376 | tf_op jit(solution)/shard_map/gather | solution.py:139
  759.8 7.1 scatter_fusion
  776.9 41.3 %collective-permute-start.2 = (f32[19,6,1,256]{3,0,2,1:T(8,128)S(1)}, f32[19,6,1,256]{3,0,2,1:T(8,128)S(1)}, u32[]{:S(2)}, u32[]{:S(2)}) collective-permute-start(f32[19,6,1,256]{3,0,2,1:T(8,128)S(1)} %get-tuple-element.121), channel_id=1, source_target_pairs={{0,2},{2,4},{4,6},{6,8},{8,10},{10,12},{12,14},{14,0},{1,3},{3,5},... | collective-permute-start | bytes 350216 | tf_op jit(solution)/shard_map/ppermute | solution.py:44
  894.9 8.3 fusion.52
  909.3 57.6 %scatter_custom_fusion.2 = f32[65536,3]{1,0:T(8,128)} fusion(s32[8192]{0:T(1024)} %bitcast.244, f32[8192,3]{1,0:T(8,128)} %bitcast_multiply_fusion, f32[]{:T(128)} %constant.108.clone.1), kind=kCustom, calls=%fused_computation.16 | custom fusion | flops 24576 | bytes 786944 | tf_op jit(solution)/shard_map/scatter-add | solution.py:158
  972.4 14.1 gather_fusion.5
  991.2 21.2 scatter_custom_fusion.3
  1013.7 649.6 %reduce-scatter.4.cloned.1.call-done = f32[4096,3]{1,0:T(8,128)} async-done(((f32[65536,3]{1,0:T(8,128)}), f32[4096,3]{1,0:T(8,128)}) %reduce-scatter.4.cloned.1.call-update) | async-done | bytes 49168
  1666.2 98.4 %all-reduce.4.cloned.1.call-done = (f32[3,4352]{1,0:T(4,128)}, f32[3,4096]{1,0:T(4,128)}) async-done(((f32[3,4352]{1,0:T(4,128)}, f32[3,4096]{1,0:T(4,128)}), (f32[3,4352]{1,0:T(4,128)}, f32[3,4096]{1,0:T(4,128)})) %all-reduce.4.cloned.1.call-update) | async-done | bytes 101392 | tf_op jit(solution)/shard_map/psum | solution.py:101
  1776.5 14.1 gather_fusion.6
  1795.3 21.2 scatter_custom_fusion.4
  1817.2 44.8 %psum.80 = f32[3,4352]{1,0:T(4,128)S(1)} all-reduce(f32[3,4352]{1,0:T(4,128)S(1)} %bitcast.231), channel_id=1, replica_groups=mesh['fx'=16,'fy'=8,'sz'=2] {'fx'}, use_global_device_ids=true, to_apply=%region_14.0 | all-reduce | flops 13056 | bytes 104448 | tf_op jit(solution)/shard_map/psum | solution.py:101
  1868.8 32.7 %all-reduce = (f32[]{:T(128)}, f32[]{:T(128)}) all-reduce(f32[]{:T(128)} %get-tuple-element.73, f32[]{:T(128)} %get-tuple-element.72), channel_id=1, replica_groups=mesh['fx'=16,'fy'=8,'sz'=2] {'fy','sz'}, use_global_device_ids=true, to_apply=%region_12.0 | all-reduce | flops 2 | bytes 16 | tf_op jit(solution)/shard_map/psum | solution.py:108
  1903.5 30.0 %psum.82 = f32[]{:T(128)} all-reduce(f32[]{:T(128)} %multiply_reduce_fusion.6), channel_id=1, replica_groups=mesh['fx'=16,'fy'=8,'sz'=2] {'fy','sz'}, use_global_device_ids=true, to_apply=%region_18.0 | all-reduce | flops 1 | bytes 8 | tf_op jit(solution)/shard_map/psum | solution.py:108
  1940.3 14.1 gather_fusion.7
  1959.1 21.2 scatter_custom_fusion.5
  1981.0 62.7 %psum.83 = f32[3,4352]{1,0:T(4,128)S(1)} all-reduce(f32[3,4352]{1,0:T(4,128)S(1)} %bitcast.232), channel_id=1, replica_groups=mesh['fx'=16,'fy'=8,'sz'=2] {'fx'}, use_global_device_ids=true, to_apply=%region_20.0 | all-reduce | flops 13056 | bytes 104448 | tf_op jit(solution)/shard_map/psum | solution.py:101
  2050.7 30.6 %psum.84 = f32[]{:T(128)} all-reduce(f32[]{:T(128)} %multiply_reduce_fusion.5), channel_id=1, replica_groups=mesh['fx'=16,'fy'=8,'sz'=2] {'fy','sz'}, use_global_device_ids=true, to_apply=%region_22.0 | all-reduce | flops 1 | bytes 8 | tf_op jit(solution)/shard_map/psum | solution.py:172
  2083.2 30.8 %psum.85 = f32[]{:T(128)} all-reduce(f32[]{:T(128)} %get-tuple-element.78), channel_id=1, replica_groups=mesh['fx'=16,'fy'=8,'sz'=2] {'fy','sz'}, use_global_device_ids=true, to_apply=%region_24.0 | all-reduce | flops 1 | bytes 8 | tf_op jit(solution)/shard_map/psum | solution.py:108
  2120.0 14.1 gather_fusion.8
  2138.8 21.2 scatter_custom_fusion.6
  2160.7 62.9 %psum.86 = f32[3,4352]{1,0:T(4,128)S(1)} all-reduce(f32[3,4352]{1,0:T(4,128)S(1)} %bitcast.233), channel_id=1, replica_groups=mesh['fx'=16,'fy'=8,'sz'=2] {'fx'}, use_global_device_ids=true, to_apply=%region_26.0 | all-reduce | flops 13056 | bytes 104448 | tf_op jit(solution)/shard_map/psum | solution.py:101
  2231.7 30.6 %psum.87 = f32[]{:T(128)} all-reduce(f32[]{:T(128)} %multiply_reduce_fusion.3), channel_id=1, replica_groups=mesh['fx'=16,'fy'=8,'sz'=2] {'fy','sz'}, use_global_device_ids=true, to_apply=%region_28.0 | all-reduce | flops 1 | bytes 8 | tf_op jit(solution)/shard_map/psum | solution.py:172
  (252 shorter events, 185.3 us)
Async XLA Ops:
  7.2 981.5 %copy-start = (f32[24,24]{1,0:T(8,128)S(1)}, f32[24,24]{1,0:T(8,128)}, u32[]{:S(2)}) copy-start(f32[24,24]{1,0:T(8,128)} %param.33) | copy-start | bytes 6916
  7.2 1656.1 %reduce-scatter.4.cloned.1.call-start = ((), (), s32[]{:S(2)}) async-start(), calls=%async_computation.1 | async-start | bytes 35651584
  769.7 4.3 collective-permute-start
  771.5 5.4 collective-permute-start.1
  776.9 44.7 %collective-permute-start.2 = (f32[19,6,1,256]{3,0,2,1:T(8,128)S(1)}, f32[19,6,1,256]{3,0,2,1:T(8,128)S(1)}, u32[]{:S(2)}, u32[]{:S(2)}) collective-permute-start(f32[19,6,1,256]{3,0,2,1:T(8,128)S(1)} %get-tuple-element.121), channel_id=1, source_target_pairs={{0,2},{2,4},{4,6},{6,8},{8,10},{10,12},{12,14},{14,0},{1,3},{3,5},... | collective-permute-start | bytes 350216 | tf_op jit(solution)/shard_map/ppermute | solution.py:44
  818.2 9.1 collective-permute-start.3
  828.1 7.8 collective-permute-start.4
  832.4 4.5 collective-permute-start.5
  863.6 5.7 collective-permute-start.6
  866.7 5.4 collective-permute-start.7
  872.1 7.0 collective-permute-start.8
  872.2 6.9 collective-permute-start.9
  880.0 4.3 collective-permute-start.10
  882.2 4.7 collective-permute-start.11
  966.9 797.6 %all-reduce.4.cloned.1.call-start = ((), (), s32[]{:S(2)}) async-start(), calls=%async_computation.2 | async-start | bytes 270336 | tf_op jit(solution)/shard_map/psum | solution.py:101
  967.7 3.9 collective-permute-start.12
  1012.4 754.1 %copy-start.5 = (f32[4096]{0:T(1024)S(1)}, f32[4096]{0:T(1024)}, u32[]{:S(2)}) copy-start(f32[4096]{0:T(1024)} %param.30) | copy-start | bytes 49156
  1765.2 5.8 collective-permute-start.13
  1772.0 3.8 collective-permute-start.14
  1862.0 6.2 collective-permute-start.15
  1934.9 4.7 collective-permute-start.16
  2043.6 6.4 collective-permute-start.17
  2115.4 4.0 collective-permute-start.18
  2223.6 6.4 collective-permute-start.19
  (36 other events, 2391.7 us)
Sparse Core Ops, SparseCore 0:
  967.1 696.1 reduce-scatter.3
  1666.3 98.2 all-reduce.3
where the time goes:
time: 2290 us; the launch traced here: 2270 us
  blocking collectives  1020 us (45%)
  waiting for transfers between devices  789 us (34%)
  other arithmetic  179 us (8%)
  local copies, waits for them, and re-layouts  167 us (7%)
  starting transfers between devices  77.1 us (3%)
    all_gather x1, blocking collectives, body(): lax.all_gather(struct_velocity, ('fy', 'sz'), axis=1, tiled=True)  697 us
    unnamed x3, waiting for transfers between devices  650 us
    psum x3, blocking collectives, apply_operator(): summed = lax.psum(summed, 'fx')  170 us
    psum x1, waiting for transfers between devices, apply_operator(): summed = lax.psum(summed, 'fx')  98.4 us
    psum x3, blocking collectives, squares(): return lax.psum(jnp.sum(vector * vector), ('fy', 'sz'))  93.5 us
    scatter-add x4, other arithmetic, apply_operator(): jax.ops.segment_sum(spread.T, conn_local.reshape(-1), num_segments=BND +...  84.9 us
    gather x8, local copies, waits for them, and re-layouts, apply_operator(): picked = extended[:, conn_local].reshape(24, -1)  65.2 us
    psum x2, blocking collectives, body(): alpha = norm_now / lax.psum(jnp.sum(direction * image), ('fy', 'sz'))  61.1 us
  transfers between devices with their start and end apart: 22, of which 18 were waited for; matrix products, arithmetic and copies ran while one was open for 2% of the time, Pallas kernels for 0%

commit v1 on v0

v1 whole, which is shorter than its diff:
```python
import jax
import jax.numpy as jnp
from jax import lax
from jax.experimental import pallas as pl
from jax.experimental.pallas import tpu as pltpu
from jax.sharding import PartitionSpec as P

F32 = jnp.float32
BF16 = jnp.bfloat16
I32 = jnp.int32
FX, FY, SZ = 16, 8, 2
OWN = 16
ITERS = 3
APPS = ITERS + 1
FORCE_SCALE = 20.0
VEL = [
    (0, 0, 0),
    (1, 0, 0),
    (-1, 0, 0),
    (0, 1, 0),
    (0, -1, 0),
    (0, 0, 1),
    (0, 0, -1),
    (1, 1, 0),
    (-1, -1, 0),
    (1, -1, 0),
    (-1, 1, 0),
    (1, 0, 1),
    (-1, 0, -1),
    (1, 0, -1),
    (-1, 0, 1),
    (0, 1, 1),
    (0, -1, -1),
    (0, 1, -1),
    (0, -1, 1),
]
X_POPS = [[i for i in range(19) if VEL[i][0] == s] for s in (1, -1)]
Y_POPS = [[i for i in range(19) if VEL[i][1] == s] for s in (1, -1)]
Z_POPS = [i for i in range(19) if VEL[i][2] != 0]
DIAGONAL = (7, 8, 9, 10)
MESH = pl.DeviceIdType.MESH


def split2(x):
    top = x.astype(BF16)
    rest = (x - top.astype(F32)).astype(BF16)
    return jnp.concatenate([top, rest], axis=0)


def dot_nt(a, b):
    return lax.dot_general(a, b, (((1,), (1,)), ((), ())), preferred_element_type=F32)


def dot_nn(a, b):
    return lax.dot_general(a, b, (((1,), (0,)), ((), ())), preferred_element_type=F32)


def exact_dot(a, b, dims=((1,), (0,))):
    return lax.dot_general(
        a, b, (dims, ((), ())), preferred_element_type=F32, precision=lax.Precision.HIGHEST
    )


def iota(shape, dim):
    return lax.broadcasted_iota(I32, shape, dim)


def group_sum(x):
    x = x + pltpu.roll(x, 64, x.ndim - 1)
    return x + pltpu.roll(x, 32, x.ndim - 1)


def send(src, dst, ssem, rsem, device):
    pltpu.make_async_remote_copy(
        src_ref=src,
        dst_ref=dst,
        send_sem=ssem,
        recv_sem=rsem,
        device_id=device,
        device_id_type=MESH,
    ).start()


def wait(ref, sem):
    pltpu.make_async_copy(ref, ref, sem).wait()


def kernel(
    pop, relax, vel, count, cell, node, weight, disp, mass, connect, modulus, basis,
    out_pop, out_sol, out_res,
    sup_send, sup_recv, wall_send, wall_recv, frc_send, frc_recv, edge_send, edge_recv,
    xs, xr, ys, yr, ds, dr, zs, zr, zxr, zys, zyr,
    rs_send, rs_recv, gh_recv, sc_send, sc_recv, ag_send, ag_recv,
    post, field, rho_ref, gain, cell_lo, cell_hi, live_ref, wallp,
    sup_lo, sup_hi, lhs, el_lo, el_hi, pick, spread, ela, vec_r, vec_p, vec_s, vec_w, vec_x,
    massc, rc, load_ref,
    s_sup, r_sup, s_wall, r_wall, s_frc, r_frc, s_edge, r_edge, s_halo, r_halo,
    s_rs, r_rs, s_gh, r_gh, s_sc, r_sc, s_ag, r_ag, s_ag2,
):
    f = lax.axis_index("fx")
    y = lax.axis_index("fy")
    z = lax.axis_index("sz")
    own = y * SZ + z

    def at_owner(o, fx=None):
        return (f if fx is None else fx, o // SZ, lax.rem(o, SZ))

    def to_owners(src_of, dst, ssem, rsem):
        def go(d, _):
            o = lax.rem(own + d, OWN)
            send(src_of(o), dst, ssem, rsem, at_owner(o))
            return 0

        lax.fori_loop(1, OWN, go, 0)

    lane = iota((1, 128), 1)
    group = lane // 32
    expand = (iota((32, 128), 0) == lax.rem(iota((32, 128), 1), 32)).astype(F32)
    quarter = (iota((16, 128), 0) // 4) == (iota((16, 128), 1) // 32)
    upper = iota((8, 128), 0) < 4

    def pack(o, _):
        def packed(x):
            x = jnp.where(quarter, exact_dot(x, expand), 0.0)
            x = x[0:8] + x[8:16]
            return x + pltpu.roll(x, 4, 0)

        tile = jnp.where(upper, packed(node[o].astype(F32)), packed(weight[o]))
        sup_send[o] = tile

        @pl.when(o == own)
        def _():
            sup_recv[o] = tile

        return 0

    lax.fori_loop(0, OWN, pack, 0)
    to_owners(lambda o: sup_send.at[o], sup_recv.at[own], s_sup, r_sup)

    for c in range(3):
        edge_send[c : c + 1, :] = disp[c : c + 1, 3840:4096]
    edge_send[3:4, :] = jnp.zeros((1, 256), F32)
    after, before = lax.rem(own + 1, OWN), lax.rem(own + OWN - 1, OWN)
    send(edge_send, edge_recv, s_edge, r_edge, at_owner(after))

    def corner(j, _):
        n = connect[pl.ds(j, 1), :]
        lo = lax.rem(n, 256)
        hi = jnp.where(n < 256, 16, n // 256 - 1)
        el_lo[j] = jnp.where(iota((256, 512), 0) == lo, 1.0, 0.0).astype(BF16)
        el_hi[j] = jnp.where(iota((24, 512), 0) == hi, 1.0, 0.0)
        return 0

    lax.fori_loop(0, 8, corner, 0)
    base = basis[...]
    gram = exact_dot(base, base, ((0,), (0,)))

    cells = cell[...]
    cell_hi16 = exact_dot((cells // 256).astype(F32), expand)
    cell_lo16 = exact_dot(lax.rem(cells, 256).astype(F32), expand)
    diag = iota((16, 16), 0) == iota((16, 16), 1)
    counts = jnp.sum(jnp.where(diag, count[...].astype(F32), 0.0), axis=1, keepdims=True)
    live16 = (lax.rem(iota((16, 128), 1), 32).astype(F32) < counts).astype(F32)
    mine = lax.rem(iota((16, 128), 0), 4) == (iota((16, 128), 1) // 32)
    fold = ((iota((8, 16), 1) // 4) == iota((8, 16), 0)).astype(F32)

    def rows_of(x):
        return exact_dot(fold, jnp.where(mine, x, 0.0))

    hi_rows, lo_rows = rows_of(cell_hi16).astype(I32), rows_of(cell_lo16).astype(I32)
    live_ref[...] = rows_of(live16)
    for g in range(4):
        at = slice(g * 128, g * 128 + 128)
        cell_lo[:, at] = jnp.where(iota((256, 128), 0) == lo_rows[g : g + 1], 1.0, 0.0).astype(BF16)
        cell_hi[:, at] = jnp.where(iota((32, 128), 0) == hi_rows[g : g + 1], 1.0, 0.0)

    def moments(fs):
        rho = fs[0]
        for i in range(1, 19):
            rho = rho + fs[i]
        mom = []
        for a in range(3):
            total = None
            for i in range(1, 19, 2):
                s = VEL[i][a]
                if s:
                    pair = fs[i] - fs[i + 1] if s > 0 else fs[i + 1] - fs[i]
                    total = pair if total is None else total + pair
            mom.append(total)
        return rho, mom

    def along(c, v):
        total = None
        for a in range(3):
            if c[a] == 1:
                total = v[a] if total is None else total + v[a]
        for a in range(3):
            if c[a] == -1:
                total = -v[a] if total is None else total - v[a]
        return total

    def collide(source):
        for k in range(4):
            fs = [source[i, k] for i in range(19)]
            om = relax[k]
            rho, mom = moments(fs)
            inv = 1.0 / rho
            u = [m * inv for m in mom]
            sq = 1.5 * (u[0] * u[0] + u[1] * u[1] + u[2] * u[2])
            rho_ref[k] = rho
            keep = 1.0 - om
            scaled = om * rho
            post[0, k] = keep * fs[0] + (1.0 / 3.0) * scaled * (1.0 - sq)
            for i in range(1, 19, 2):
                t = (1.0 / 18.0) if i < 7 else (1.0 / 36.0)
                a = along(VEL[i], u)
                ts = t * scaled
                even = ts * (1.0 + 4.5 * a * a - sq)
                odd = ts * (3.0 * a)
                post[i, k] = keep * fs[i] + (even + odd)
                post[i + 1, k] = keep * fs[i + 1] + (even - odd)

    def turn(i, v):
        cy, cz = VEL[i][1], VEL[i][2]
        if cy:
            v = pltpu.roll(v, cy % 8, 0)
        if cz:
            v = pltpu.roll(v, cz % 256, 1)
        return v

    lane8 = iota((8, 128), 1)
    row8 = iota((8, 128), 0)

    def stream(step, target, wall_gain):
        for k in range(4):
            for c in range(3):
                gain[c, k] = wall_gain[c][k] * rho_ref[k] * (1.0 / 6.0)
        for x in range(4):
            zpack = jnp.zeros((8, 128), F32)
            for i in range(19):
                cx, cy, cz = VEL[i]
                k = (x - cx) % 4
                v = post[i, k]
                if i:
                    push = along(VEL[i], [gain[c, k] for c in range(3)])
                    v = v + (2.0 * push if i < 7 else push)
                v = turn(i, v)
                if k != x - cx:
                    side = 0 if cx > 0 else 1
                    xs[step, side, X_POPS[side].index(i)] = v
                    if cy:
                        r = 0 if cy > 0 else 7
                        ds[step, DIAGONAL.index(i)] = v[r : r + 1, :]
                else:
                    target[i, x] = v
                if cy:
                    side = 0 if cy > 0 else 1
                    r = 0 if cy > 0 else 7
                    ys[step, side, Y_POPS[side].index(i), x : x + 1, :] = v[r : r + 1, :]
                if cz:
                    col = v[:, 0:1] if cz > 0 else v[:, 255:256]
                    zpack = jnp.where(lane8 == Z_POPS.index(i), col, zpack)
            zs[step, x] = zpack
            zys[step, 0, x : x + 1, :] = zpack[0:1, :]
            zys[step, 1, x : x + 1, :] = zpack[7:8, :]
        xp, xm = lax.rem(f + 1, FX), lax.rem(f + FX - 1, FX)
        yp, ym = lax.rem(y + 1, FY), lax.rem(y + FY - 1, FY)
        zo = 1 - z
        jobs = [
            (xs.at[step, 0], xr.at[step, 0], (xp, y, z)),
            (xs.at[step, 1], xr.at[step, 1], (xm, y, z)),
            (ys.at[step, 0], yr.at[step, 0], (f, yp, z)),
            (ys.at[step, 1], yr.at[step, 1], (f, ym, z)),
            (zs.at[step], zr.at[step], (f, y, zo)),
            (ds.at[step, 0], dr.at[step, 0], (xp, yp, z)),
            (ds.at[step, 1], dr.at[step, 1], (xm, ym, z)),
            (ds.at[step, 2], dr.at[step, 2], (xp, ym, z)),
            (ds.at[step, 3], dr.at[step, 3], (xm, yp, z)),
            (zs.at[step, 0], zxr.at[step, 0], (xp, y, zo)),
            (zs.at[step, 3], zxr.at[step, 1], (xm, y, zo)),
            (zys.at[step, 0], zyr.at[step, 0], (f, yp, zo)),
            (zys.at[step, 1], zyr.at[step, 1], (f, ym, zo)),
        ]
        for n, (src, dst, device) in enumerate(jobs):
            send(src, dst, s_halo.at[step, n], r_halo.at[step, n], device)
        for n, (src, dst, device) in enumerate(jobs):
            wait(dst, r_halo.at[step, n])
        for side in range(2):
            for n, i in enumerate(X_POPS[side]):
                target[i, 0 if side == 0 else 3] = xr[step, side, n]
        for side in range(2):
            r = 0 if side == 0 else 7
            for n, i in enumerate(Y_POPS[side]):
                cx = VEL[i][0]
                for x in range(4):
                    if 0 <= x - cx <= 3:
                        target[i, x, r : r + 1, :] = yr[step, side, n, x : x + 1, :]
        for n, i in enumerate(DIAGONAL):
            cx, cy, _ = VEL[i]
            r = 0 if cy > 0 else 7
            target[i, 0 if cx > 0 else 3, r : r + 1, :] = dr[step, n]
        z11, z12, z13, z14, z15, z16, z17, z18 = [Z_POPS.index(i) for i in range(11, 19)]
        for x in range(4):
            zin = zr[step, x]
            if x == 0:
                zin = jnp.where((lane8 == z11) | (lane8 == z13), zxr[step, 0], zin)
            if x == 3:
                zin = jnp.where((lane8 == z12) | (lane8 == z14), zxr[step, 1], zin)
            low = (row8 == 0) & ((lane8 == z15) | (lane8 == z17))
            high = (row8 == 7) & ((lane8 == z16) | (lane8 == z18))
            zin = jnp.where(low, zyr[step, 0, x : x + 1, :], zin)
            zin = jnp.where(high, zyr[step, 1, x : x + 1, :], zin)
            for n, i in enumerate(Z_POPS):
                col = zin[:, n : n + 1]
                if VEL[i][2] > 0:
                    target[i, x, :, 0:128] = jnp.where(lane8 == 0, col, target[i, x, :, 0:128])
                else:
                    target[i, x, :, 128:256] = jnp.where(
                        lane8 == 127, col, target[i, x, :, 128:256]
                    )
        return jobs

    collide(pop)

    wait(sup_recv.at[pl.ds(0, OWN - 1)], r_sup)

    def supports(b, _):
        for r in range(4):
            n = sup_recv[b, r : r + 1, :].astype(I32)
            w = sup_recv[b, r + 4 : r + 5, :]
            sup_lo[b, :, r * 128 : r * 128 + 128] = jnp.where(
                iota((256, 128), 0) == lax.rem(n, 256), 1.0, 0.0
            ).astype(BF16)
            sup_hi[b, :, r * 128 : r * 128 + 128] = jnp.where(
                iota((16, 128), 0) == n // 256, w, 0.0
            )
        return 0

    lax.fori_loop(0, OWN, supports, 0)
    for c in range(3):
        for h in range(16):
            load_ref[c * 16 + h : c * 16 + h + 1, :] = vel[c : c + 1, h * 256 : h * 256 + 256]
    table = split2(load_ref[...])

    def answer(b, _):
        out = dot_nn(table, sup_lo[b])
        out = out[0:48] + out[48:96]
        hot = sup_hi[b]
        rows = []
        for c in range(3):
            m = out[c * 16 : c * 16 + 16] * hot
            m = m[:, 0:128] + m[:, 128:256] + m[:, 256:384] + m[:, 384:512]
            rows.append(jnp.sum(m, axis=0, keepdims=True))
        rows.append(jnp.zeros((1, 128), F32))
        for c in range(4):
            wall_send[b, c : c + 1, :] = rows[c]
        return 0

    lax.fori_loop(0, OWN, answer, 0)
    wall_recv[own] = wall_send[own]
    to_owners(lambda o: wall_send.at[o], wall_recv.at[own], s_wall, r_wall)

    def elements(values):
        both = split2(values)

        def gather(j, _):
            out = dot_nn(both, el_lo[j])
            out = out[0:80] + out[80:160]
            hot = el_hi[j]
            for c in range(3):
                pick[pl.ds(c * 8 + j, 1), :] = jnp.sum(
                    out[c * 24 : c * 24 + 24] * hot, axis=0, keepdims=True
                )
            return 0

        lax.fori_loop(0, 8, gather, 0)
        picked = pick[...]
        spread[...] = exact_dot(gram, picked) * modulus[...]
        ela[...] = jnp.zeros((160, 256), F32)

        def scatter(j, _):
            hot = el_hi[j]
            parts = [hot * spread[pl.ds(c * 8 + j, 1), :] for c in range(3)]
            parts.append(jnp.zeros((8, 512), F32))
            ela[...] += dot_nt(split2(jnp.concatenate(parts, axis=0)), el_lo[j])
            return 0

        lax.fori_loop(0, 8, scatter, 0)
        return ela[0:80] + ela[80:160], picked

    wait(edge_recv, r_edge)
    vec_r[...] = jnp.zeros((80, 256), F32)
    has_before = (own > 0).astype(F32)
    has_after = (own < OWN - 1).astype(F32)
    for c in range(3):
        for h in range(16):
            row = disp[c : c + 1, h * 256 : h * 256 + 256]
            vec_r[c * 24 + h : c * 24 + h + 1, :] = row
            vec_x[c * 16 + h : c * 16 + h + 1, :] = row
        vec_r[c * 24 + 16 : c * 24 + 17, :] = edge_recv[c : c + 1, :] * has_before
    vec_w[...] = elements(vec_r[...])[0]
    massc[:, 0:128] = mass[pl.ds(2 * f, 1), :]
    massc[:, 128:256] = mass[pl.ds(2 * f + 1, 1), :]

    wait(wall_recv.at[pl.ds(0, OWN - 1)], r_wall)
    wall = [None] * 4
    for g in range(4):
        total = jnp.zeros((4, 128), F32)
        for q in range(4):
            total = jnp.where(group == q, group_sum(wall_recv[g * 4 + q]), total)
        wall[g] = total * live_ref[g : g + 1, :]
    for g in range(4):
        hot = cell_hi[:, g * 128 : g * 128 + 128]
        parts = [hot * wall[g][c : c + 1, :] for c in range(3)]
        wallp[:, g * 128 : g * 128 + 128] = split2(jnp.concatenate(parts, axis=0))
    summed = dot_nt(wallp[...], cell_lo[...])
    summed = summed[0:96] + summed[96:192]
    wall_gain = [
        [summed[c * 32 + k * 8 : c * 32 + k * 8 + 8, :] for k in range(4)] for c in range(3)
    ]

    jobs0 = stream(0, field, wall_gain)
    collide(field)
    jobs1 = stream(1, out_pop, wall_gain)

    rows = [[], [], [], []]
    for k in range(4):
        rho, mom = moments([out_pop[i, k] for i in range(19)])
        for q, part in enumerate([rho] + mom):
            rows[q].append(part)
    values = jnp.concatenate([r for q in range(4) for r in rows[q]], axis=0)
    at_slots = dot_nn(split2(values), cell_lo[...])
    at_slots = at_slots[0:128] + at_slots[128:256]
    hot = cell_hi[...]
    slot = [
        jnp.sum(at_slots[q * 32 : q * 32 + 32] * hot, axis=0, keepdims=True) for q in range(4)
    ]
    row4 = iota((4, 128), 0)
    for g in range(4):
        at = slice(g * 128, g * 128 + 128)
        mom = jnp.zeros((4, 128), F32)
        for c in range(3):
            mom = jnp.where(row4 == c, slot[c + 1][:, at], mom)
        force = (mom - slot[0][:, at] * wall[g]) * live_ref[g : g + 1, :]
        for q in range(4):
            frc_send[g * 4 + q] = group_sum(jnp.where(group == q, force, 0.0))
    frc_recv[own] = frc_send[own]
    to_owners(lambda o: frc_send.at[o], frc_recv.at[own], s_frc, r_frc)
    wait(frc_recv.at[pl.ds(0, OWN - 1)], r_frc)

    load_ref[...] = jnp.zeros((48, 256), F32)

    def collect(b, _):
        force = frc_recv[b]
        parts = []
        for c in range(3):
            line = force[c : c + 1, :]
            line = jnp.concatenate([line] * 4, axis=1)
            parts.append(sup_hi[b] * line)
        got = dot_nt(split2(jnp.concatenate(parts, axis=0)), sup_lo[b])
        load_ref[...] += got[0:48] + got[48:96]
        return 0

    lax.fori_loop(0, OWN, collect, 0)

    row4w = iota((4, 256), 0)

    def exchange(app, sums, with_mass):
        for c in range(3):
            for h in range(17):
                rs_send[app, h, c : c + 1, :] = sums[c * 24 + h : c * 24 + h + 1, :]
        for h in range(17):
            rs_send[app, h, 3:4, :] = jnp.zeros((1, 256), F32)
        rs_recv[app, f] = rs_send[app, f]

        def go(d, _):
            j = lax.rem(f + d, FX)
            send(rs_send.at[app, j], rs_recv.at[app, f], s_rs.at[app], r_rs.at[app], (j, y, z))
            return 0

        lax.fori_loop(1, FX, go, 0)
        send(
            rs_send.at[app, 16], gh_recv.at[app, f], s_gh.at[app], r_gh.at[app],
            at_owner(before, FX - 1),
        )
        if with_mass is not None:
            to_owners(lambda o: sc_send.at[app], sc_recv.at[app, own], s_sc.at[app], r_sc.at[app])
        wait(rs_recv.at[app, pl.ds(0, FX - 1)], r_rs.at[app])
        total = rs_recv[app, 0]
        for n in range(1, FX):
            total = total + rs_recv[app, n]
        ag_send[app] = total

        @pl.when(f == FX - 1)
        def _():
            wait(gh_recv.at[app], r_gh.at[app])
            extra = gh_recv[app, 0]
            for n in range(1, FX):
                extra = extra + gh_recv[app, n]
            ag_send[app] = ag_send[app] + extra * has_after

        if with_mass is not None:
            wait(sc_recv.at[app, pl.ds(0, OWN - 1)], r_sc.at[app])
            part = sc_recv[app, 0]
            for n in range(1, OWN):
                part = part + sc_recv[app, n]
            mine = ag_send[app] + with_mass
            ag_send[app] = jnp.where(row4w == 3, jnp.concatenate([part, part], axis=1), mine)
        ag_recv[app, f] = ag_send[app]

        def spread_out(d, _):
            j = lax.rem(f + d, FX)
            send(ag_send.at[app], ag_recv.at[app, f], s_ag.at[app], r_ag.at[app], (j, y, z))
            return 0

        lax.fori_loop(1, FX, spread_out, 0)

        @pl.when(f == FX - 1)
        def _():
            def onward(j, _):
                send(
                    ag_send.at[app], ag_recv.at[app, 16], s_ag2.at[app], r_ag.at[app],
                    at_owner(after, j),
                )
                return 0

            lax.fori_loop(0, FX, onward, 0)

        wait(ag_recv.at[app, pl.ds(0, FX)], r_ag.at[app])

    def gathered(app, target):
        for c in range(3):
            for h in range(16):
                target[c * 24 + h : c * 24 + h + 1, :] = ag_recv[app, h, c : c + 1, :]
            target[c * 24 + 16 : c * 24 + 17, :] = ag_recv[app, 16, c : c + 1, :] * has_before

    kdisp = vec_w[...]
    pad8 = jnp.zeros((8, 256), F32)
    loads = []
    for c in range(3):
        loads += [FORCE_SCALE * load_ref[c * 16 : c * 16 + 16, :], pad8]
    loads.append(pad8)
    exchange(0, jnp.concatenate(loads, axis=0) - kdisp, None)
    gathered(0, vec_r)
    vec_p[...] = jnp.zeros((80, 256), F32)
    vec_s[...] = jnp.zeros((80, 256), F32)
    vec_w[...] = jnp.zeros((80, 256), F32)

    def iteration(app, carry):
        alpha, gamma = carry
        sums, picked = elements(vec_r[...])
        for c in range(3):
            rc[c : c + 1, :] = vec_r[pl.ds(c * 24 + f, 1), :]
        rc[3:4, :] = jnp.zeros((1, 256), F32)
        chunk = rc[...]
        weighted = massc[...] * chunk
        mine = jnp.sum(chunk * chunk, keepdims=True)
        energy = jnp.sum(picked * spread[...], keepdims=True) + jnp.sum(
            weighted * chunk, keepdims=True
        )
        scalars = jnp.where(lane == 0, mine, jnp.where(lane == 1, energy, 0.0))
        sc_send[app] = scalars
        sc_recv[app, own] = scalars
        exchange(app, sums, weighted)
        gathered(app, vec_w)
        both = ag_recv[app, 0]
        for n in range(1, FX):
            both = both + ag_recv[app, n]
        new = both[3:4, 0:1]
        delta = both[3:4, 1:2]
        beta = jnp.where(app == 1, 0.0, new / gamma)
        alpha = new / (delta - beta * new / alpha)
        p = vec_r[...] + beta * vec_p[...]
        s = vec_w[...] + beta * vec_s[...]
        vec_p[...] = p
        vec_s[...] = s
        vec_r[...] = vec_r[...] - alpha * s
        for c in range(3):
            vec_x[c * 16 : c * 16 + 16, :] += alpha * p[c * 24 : c * 24 + 16, :]
        return alpha, new

    one = jnp.ones((1, 1), F32)
    lax.fori_loop(1, APPS, iteration, (one, one))

    for c in range(3):
        for h in range(16):
            at = slice(h * 256, h * 256 + 256)
            out_sol[c : c + 1, at] = vec_x[c * 16 + h : c * 16 + h + 1, :]
            out_res[c : c + 1, at] = vec_r[c * 24 + h : c * 24 + h + 1, :]

    wait(sup_recv.at[pl.ds(0, OWN - 1)], s_sup)
    wait(edge_send, s_edge)
    wait(wall_recv.at[pl.ds(0, OWN - 1)], s_wall)
    wait(frc_recv.at[pl.ds(0, OWN - 1)], s_frc)
    for step, jobs in enumerate((jobs0, jobs1)):
        for n, (src, dst, device) in enumerate(jobs):
            wait(src, s_halo.at[step, n])
    for app in range(APPS):
        wait(rs_recv.at[app, pl.ds(0, FX - 1)], s_rs.at[app])
        wait(rs_send.at[app, 16], s_gh.at[app])
        if app:
            wait(sc_recv.at[app, pl.ds(0, OWN - 1)], s_sc.at[app])
        wait(ag_recv.at[app, pl.ds(0, FX - 1)], s_ag.at[app])

        @pl.when(f == FX - 1)
        def _():
            wait(ag_recv.at[app, pl.ds(0, FX)], s_ag2.at[app])


SCRATCH = dict(
    sup_send=(16, 8, 128), sup_recv=(16, 8, 128),
    wall_send=(16, 4, 128), wall_recv=(16, 4, 128),
    frc_send=(16, 4, 128), frc_recv=(16, 4, 128),
    edge_send=(4, 256), edge_recv=(4, 256),
    xs=(2, 2, 5, 8, 256), xr=(2, 2, 5, 8, 256),
    ys=(2, 2, 5, 4, 256), yr=(2, 2, 5, 4, 256),
    ds=(2, 4, 1, 256), dr=(2, 4, 1, 256),
    zs=(2, 4, 8, 128), zr=(2, 4, 8, 128), zxr=(2, 2, 8, 128),
    zys=(2, 2, 4, 128), zyr=(2, 2, 4, 128),
    rs_send=(APPS, 17, 4, 256), rs_recv=(APPS, 16, 4, 256), gh_recv=(APPS, 16, 4, 256),
    sc_send=(APPS, 1, 128), sc_recv=(APPS, 16, 1, 128),
    ag_send=(APPS, 4, 256), ag_recv=(APPS, 17, 4, 256),
    post=(19, 4, 8, 256), field=(19, 4, 8, 256), rho_ref=(4, 8, 256), gain=(3, 4, 8, 256),
    cell_lo=((256, 512), BF16), cell_hi=(32, 512), live_ref=(8, 128), wallp=((192, 512), BF16),
    sup_lo=((16, 256, 512), BF16), sup_hi=(16, 16, 512), lhs=(8, 128),
    el_lo=((8, 256, 512), BF16), el_hi=(8, 24, 512),
    pick=(24, 512), spread=(24, 512), ela=(160, 256),
    vec_r=(80, 256), vec_p=(80, 256), vec_s=(80, 256), vec_w=(80, 256), vec_x=(48, 256),
    massc=(1, 256), rc=(4, 256), load_ref=(48, 256),
)


def scratch_shapes():
    shapes = []
    for shape in SCRATCH.values():
        kind = F32
        if isinstance(shape[0], tuple):
            shape, kind = shape
        shapes.append(pltpu.VMEM(shape, kind))
    dma = pltpu.SemaphoreType.DMA
    shapes += [dma] * 8 + [dma((2, 13))] * 2 + [dma((APPS,))] * 9
    return shapes


def body(
    populations, relaxation, struct_velocity, iface_count, iface_cell, rbf_node, rbf_weight,
    disp_prev, node_mass, connect, modulus, strain_basis,
):
    vmem = pl.BlockSpec(memory_space=pltpu.VMEM)
    return pl.pallas_call(
        kernel,
        out_shape=(
            jax.ShapeDtypeStruct(populations.shape, F32),
            jax.ShapeDtypeStruct(disp_prev.shape, F32),
            jax.ShapeDtypeStruct(disp_prev.shape, F32),
        ),
        in_specs=[vmem] * 12,
        out_specs=(vmem, vmem, vmem),
        scratch_shapes=scratch_shapes(),
        compiler_params=pltpu.CompilerParams(
            has_side_effects=True, vmem_limit_bytes=48 * 1024 * 1024
        ),
        name="window",
    )(
        populations,
        relaxation,
        struct_velocity,
        iface_count.reshape(1, 16),
        iface_cell.reshape(16, 32),
        rbf_node.reshape(16, 16, 32),
        rbf_weight.reshape(16, 16, 32),
        disp_prev,
        node_mass.reshape(32, 128),
        connect.reshape(8, 512),
        modulus.reshape(1, 512),
        strain_basis,
    )


def solution(mesh):
    return jax.shard_map(
        body,
        mesh=mesh,
        in_specs=(
            P(None, "fx", "fy", "sz"),
            P("fx", "fy", "sz"),
            P(None, ("fy", "sz")),
            P("fx", "fy", "sz", None),
            P("fx", "fy", "sz", None, None),
            P("fx", "fy", "sz", None, None, None),
            P("fx", "fy", "sz", None, None, None),
            P(None, ("fy", "sz")),
            P(("fy", "sz")),
            P("fx", ("fy", "sz"), None, None),
            P("fx", ("fy", "sz"), None),
            P(),
        ),
        out_specs=(P(None, "fx", "fy", "sz"), P(None, ("fy", "sz")), P(None, ("fy", "sz"))),
        check_vma=False,
    )
```

time: 2290 us -> 134 us (0.06)
  blocking collectives: 1020 us -> 0 us
  waiting for transfers between devices: 789 us -> 0 us
  other arithmetic: 179 us -> 0 us
  local copies, waits for them, and re-layouts: 167 us -> 10.9 us
  Pallas kernels: 0 us -> 122 us
  starting transfers between devices: 77.1 us -> 0 us
    all_gather x1 -> x0, blocking collectives: 697 us -> none  [body(): lax.all_gather(struct_velocity, ('fy', 'sz'), axis=1, tiled=True)]
    unnamed x3 -> x0, waiting for transfers between devices: 650 us -> none
    psum x8 -> x0, blocking collectives: 325 us -> none  [the longest x3 170 us: apply_operator(): summed = lax.psum(summed, 'fx')]
    scatter-add x11 -> x0, other arithmetic: 157 us -> none  [the longest x4 84.9 us: apply_operator(): jax.ops.segment_sum(spread.T, conn_local.reshape(-1), num_segments=BND +...]
    pallas_call x0 -> x1, Pallas kernels: none -> 122 us  [body(): pl.pallas_call(kernel, out_shape=(jax.ShapeDtypeStruct(populations.shape,...]
    gather x13 -> x0, local copies, waits for them, and re-layouts: 116 us -> none  [the longest x8 65.2 us: apply_operator(): picked = extended[:, conn_local].reshape(24, -1)]
    psum x1 -> x0, waiting for transfers between devices: 98.4 us -> none  [apply_operator(): summed = lax.psum(summed, 'fx')]
    ppermute x20 -> x0, starting transfers between devices: 77.1 us -> none  [the longest x6 51.8 us: with_halo(): before = lax.ppermute(last, axis, up)]
  transfers between devices with their start and end apart: 22 -> 0, of which waited for: 18 -> 0; matrix products, arithmetic and copies ran while one was open for 2% -> 0% of each run, Pallas kernels for 0% -> 0%
where the time goes in v1:
time: 134 us; the launch traced here: 133 us
  Pallas kernels  122 us (91%)
  local copies, waits for them, and re-layouts  10.9 us (8%)
    pallas_call x1, Pallas kernels, body(): pl.pallas_call(kernel, out_shape=(jax.ShapeDtypeStruct(populations.shape,...  122 us
    unnamed x27, local copies, waits for them, and re-layouts  10.9 us

profile of v1, /device:TPU:1, one launch (start us, length us, event | category | flops | bytes accessed | tf_op | source)
XLA Modules:
  0.0 133.4 jit_solution(6674005256401286147)
XLA Ops:
  0.6 0.0 copy-start.8
  0.6 0.0 copy-start.11
  0.7 0.7 copy-done.8
  1.3 0.0 copy-done.11
  1.3 0.0 copy-start
  1.3 1.1 copy-done
  2.4 0.0 copy-start.1
  2.4 0.9 copy-done.1
  3.3 0.0 copy-start.2
  3.3 0.9 copy-done.2
  4.2 0.0 copy-start.3
  4.2 0.8 copy-done.3
  5.1 0.0 copy-start.4
  5.1 0.8 copy-done.4
  5.9 0.0 copy-start.5
  5.9 0.8 copy-done.5
  6.7 0.7 copy-done.6
  7.4 0.7 copy-done.7
  8.1 0.7 copy-done.9
  8.8 0.7 copy-done.10
  9.5 121.8 %window.1 = (f32[19,4,8,256]{3,2,1,0:T(8,128)S(1)}, f32[3,4096]{1,0:T(4,128)S(1)}, f32[3,4096]{1,0:T(4,128)S(1)}) custom-call(f32[19,4,8,256]{3,2,1,0:T(8,128)S(1)} %copy-done, f32[4,8,256]{2,1,0:T(8,128)S(1)} %copy-done.5, f32[3,4096]{1,0:T(4,128)S(1)} %copy-done.3, s32[1,16]{1,0:T(1,128)S(1)} %bitcast.13, s32[16,32]{1,0:T(8,128)S(1)} %bitcast.11, ...), custom_call_target="tpu_custom_call" | custom-call | tf_op jit(solution)/shard_map/window/pallas_call | solution.py:650
  131.3 0.8 copy.18
  132.1 0.6 copy.19
  132.8 0.6 copy.20
  (4 shorter events, 0.0 us)
Async XLA Ops:
  0.6 0.7 copy-start.8
  0.6 0.7 copy-start.11
  1.3 1.1 copy-start
  2.4 0.9 copy-start.1
  3.3 0.9 copy-start.2
  4.2 0.8 copy-start.3
  5.1 0.8 copy-start.4
  5.9 0.8 copy-start.5
  6.7 0.7 copy-start.6
  7.4 0.7 copy-start.7
  8.1 0.7 copy-start.9
  8.8 0.7 copy-start.10

commit v2 on v1

--- a/solution.py
+++ b/solution.py
@@ -39,6 +39,14 @@
 Z_POPS = [i for i in range(19) if VEL[i][2] != 0]
 DIAGONAL = (7, 8, 9, 10)
 MESH = pl.DeviceIdType.MESH
+FAR_X = (8, 7, 9, 6, 10, 5, 11, 4, 12, 3, 13, 2, 14, 1, 15)
+FAR_OWN = (
+    (4, 1), (2, 1), (6, 1), (3, 1), (5, 1), (3, 0), (5, 0), (4, 0),
+    (1, 1), (7, 1), (0, 1), (1, 0), (7, 0), (2, 0), (6, 0),
+)
+HIGH_RELAYS = (15, 7)
+LOW_RELAYS = (14, 6)
+INPUTS = 12
 
 
 def split2(x):
@@ -81,21 +89,50 @@
     ).start()
 
 
+def greet(f, y, z, own):
+    sem = pltpu.get_barrier_semaphore()
+
+    def tell(device):
+        pl.semaphore_signal(sem, inc=1, device_id=device, device_id_type=MESH)
+
+    for d in FAR_X:
+        tell((lax.rem(f + d, FX), y, z))
+    for dy, dz in FAR_OWN:
+        tell((f, lax.rem(y + dy, FY), lax.rem(z + dz, SZ)))
+    for dx in (1, FX - 1):
+        tell((lax.rem(f + dx, FX), y, 1 - z))
+        for dy in (1, FY - 1):
+            tell((lax.rem(f + dx, FX), lax.rem(y + dy, FY), z))
+    for relays, step in ((HIGH_RELAYS, 1), (LOW_RELAYS, OWN - 1)):
+        there = lax.rem(own + step, OWN)
+
+        for relay, first in zip(relays, (12, 4)):
+
+            @pl.when(f == relay)
+            def _():
+                for n in range(8):
+                    tell(((first + n) % FX, there // SZ, lax.rem(there, SZ)))
+
+    pl.semaphore_wait(sem, 15 + 15 + 6 + 2)
+
+
 def wait(ref, sem):
     pltpu.make_async_copy(ref, ref, sem).wait()
 
 
 def kernel(
+    pop_h, relax_h, vel_h, count_h, cell_h, node_h, weight_h, disp_h, mass_h, connect_h,
+    modulus_h, basis_h,
+    out_pop, out_sol, out_res,
     pop, relax, vel, count, cell, node, weight, disp, mass, connect, modulus, basis,
-    out_pop, out_sol, out_res,
     sup_send, sup_recv, wall_send, wall_recv, frc_send, frc_recv, edge_send, edge_recv,
     xs, xr, ys, yr, ds, dr, zs, zr, zxr, zys, zyr,
-    rs_send, rs_recv, gh_recv, sc_send, sc_recv, ag_send, ag_recv,
+    rs_send, rs_recv, rl_recv, sc_send, sc_recv, ag_send, ag_recv,
     post, field, rho_ref, gain, cell_lo, cell_hi, live_ref, wallp,
-    sup_lo, sup_hi, lhs, el_lo, el_hi, pick, spread, ela, vec_r, vec_p, vec_s, vec_w, vec_x,
-    massc, rc, load_ref,
+    sup_lo, sup_hi, el_lo, el_hi, pick, spread, vec_r, vec_p, vec_s, vec_w, vec_x,
+    massx, rc, load_ref, s_in,
     s_sup, r_sup, s_wall, r_wall, s_frc, r_frc, s_edge, r_edge, s_halo, r_halo,
-    s_rs, r_rs, s_gh, r_gh, s_sc, r_sc, s_ag, r_ag, s_ag2,
+    s_rs, r_rs, s_rl, r_rl, s_sc, r_sc, s_ag, r_ag, s_ag2,
 ):
     f = lax.axis_index("fx")
     y = lax.axis_index("fy")
@@ -106,55 +143,66 @@
         return (f if fx is None else fx, o // SZ, lax.rem(o, SZ))
 
     def to_owners(src_of, dst, ssem, rsem):
-        def go(d, _):
-            o = lax.rem(own + d, OWN)
-            send(src_of(o), dst, ssem, rsem, at_owner(o))
-            return 0
-
-        lax.fori_loop(1, OWN, go, 0)
+        for dy, dz in FAR_OWN:
+            there = (f, lax.rem(y + dy, FY), lax.rem(z + dz, SZ))
+            send(src_of(there[1] * SZ + there[2]), dst, ssem, rsem, there)
+
+    inputs = [
+        (node_h, node), (weight_h, weight), (disp_h, disp), (mass_h, mass), (connect_h, connect),
+        (basis_h, basis), (cell_h, cell), (count_h, count), (pop_h, pop), (relax_h, relax),
+        (vel_h, vel), (modulus_h, modulus),
+    ]
+    copies = [pltpu.make_async_copy(a, b, s_in.at[n]) for n, (a, b) in enumerate(inputs)]
+    for copy in copies:
+        copy.start()
 
     lane = iota((1, 128), 1)
     group = lane // 32
     expand = (iota((32, 128), 0) == lax.rem(iota((32, 128), 1), 32)).astype(F32)
-    quarter = (iota((16, 128), 0) // 4) == (iota((16, 128), 1) // 32)
+    quarter = (lax.rem(iota((256, 128), 0), 16) // 4) == (iota((256, 128), 1) // 32)
     upper = iota((8, 128), 0) < 4
-
-    def pack(o, _):
-        def packed(x):
-            x = jnp.where(quarter, exact_dot(x, expand), 0.0)
-            x = x[0:8] + x[8:16]
-            return x + pltpu.roll(x, 4, 0)
-
-        tile = jnp.where(upper, packed(node[o].astype(F32)), packed(weight[o]))
-        sup_send[o] = tile
-
-        @pl.when(o == own)
-        def _():
-            sup_recv[o] = tile
-
-        return 0
-
-    lax.fori_loop(0, OWN, pack, 0)
+    copies[0].wait()
+    copies[1].wait()
+    spread_n = exact_dot(node[...].astype(F32).reshape(256, 32), expand)
+    spread_w = exact_dot(weight[...].reshape(256, 32), expand)
+    spread_n = jnp.where(quarter, spread_n, 0.0)
+    spread_w = jnp.where(quarter, spread_w, 0.0)
+
+    def packed(x, o):
+        x = x[o * 16 : o * 16 + 8] + x[o * 16 + 8 : o * 16 + 16]
+        return x + pltpu.roll(x, 4, 0)
+
+    for o in range(OWN):
+        sup_send[o] = jnp.where(upper, packed(spread_n, o), packed(spread_w, o))
+    sup_recv[own] = sup_send[own]
+    greet(f, y, z, own)
     to_owners(lambda o: sup_send.at[o], sup_recv.at[own], s_sup, r_sup)
 
+    copies[2].wait()
+    copies[3].wait()
     for c in range(3):
         edge_send[c : c + 1, :] = disp[c : c + 1, 3840:4096]
-    edge_send[3:4, :] = jnp.zeros((1, 256), F32)
+    massx[...] = jnp.zeros((24, 256), F32)
+    for h in range(16):
+        massx[h : h + 1, 0:128] = mass[2 * h : 2 * h + 1, :]
+        massx[h : h + 1, 128:256] = mass[2 * h + 1 : 2 * h + 2, :]
+    edge_send[3:4, :] = massx[15:16, :]
     after, before = lax.rem(own + 1, OWN), lax.rem(own + OWN - 1, OWN)
     send(edge_send, edge_recv, s_edge, r_edge, at_owner(after))
 
-    def corner(j, _):
-        n = connect[pl.ds(j, 1), :]
+    copies[4].wait()
+    copies[5].wait()
+    for j in range(8):
+        n = connect[j : j + 1, :]
         lo = lax.rem(n, 256)
         hi = jnp.where(n < 256, 16, n // 256 - 1)
         el_lo[j] = jnp.where(iota((256, 512), 0) == lo, 1.0, 0.0).astype(BF16)
         el_hi[j] = jnp.where(iota((24, 512), 0) == hi, 1.0, 0.0)
-        return 0
-
-    lax.fori_loop(0, 8, corner, 0)
     base = basis[...]
     gram = exact_dot(base, base, ((0,), (0,)))
 
+    copies[6].wait()
+    copies[7].wait()
     cells = cell[...]
     cell_hi16 = exact_dot((cells // 256).astype(F32), expand)
     cell_lo16 = exact_dot(lax.rem(cells, 256).astype(F32), expand)
@@ -267,11 +315,6 @@
         yp, ym = lax.rem(y + 1, FY), lax.rem(y + FY - 1, FY)
         zo = 1 - z
         jobs = [
-            (xs.at[step, 0], xr.at[step, 0], (xp, y, z)),
-            (xs.at[step, 1], xr.at[step, 1], (xm, y, z)),
-            (ys.at[step, 0], yr.at[step, 0], (f, yp, z)),
-            (ys.at[step, 1], yr.at[step, 1], (f, ym, z)),
-            (zs.at[step], zr.at[step], (f, y, zo)),
             (ds.at[step, 0], dr.at[step, 0], (xp, yp, z)),
             (ds.at[step, 1], dr.at[step, 1], (xm, ym, z)),
             (ds.at[step, 2], dr.at[step, 2], (xp, ym, z)),
@@ -280,6 +323,11 @@
             (zs.at[step, 3], zxr.at[step, 1], (xm, y, zo)),
             (zys.at[step, 0], zyr.at[step, 0], (f, yp, zo)),
             (zys.at[step, 1], zyr.at[step, 1], (f, ym, zo)),
+            (zs.at[step], zr.at[step], (f, y, zo)),
+            (ys.at[step, 0], yr.at[step, 0], (f, yp, z)),
+            (ys.at[step, 1], yr.at[step, 1], (f, ym, z)),
+            (xs.at[step, 0], xr.at[step, 0], (xp, y, z)),
+            (xs.at[step, 1], xr.at[step, 1], (xm, y, z)),
         ]
         for n, (src, dst, device) in enumerate(jobs):
             send(src, dst, s_halo.at[step, n], r_halo.at[step, n], device)
@@ -320,11 +368,13 @@
                     )
         return jobs
 
+    copies[8].wait()
+    copies[9].wait()
     collide(pop)
 
     wait(sup_recv.at[pl.ds(0, OWN - 1)], r_sup)
 
-    def supports(b, _):
+    for b in range(OWN):
         for r in range(4):
             n = sup_recv[b, r : r + 1, :].astype(I32)
             w = sup_recv[b, r + 4 : r + 5, :]
@@ -334,15 +384,14 @@
             sup_hi[b, :, r * 128 : r * 128 + 128] = jnp.where(
                 iota((16, 128), 0) == n // 256, w, 0.0
             )
-        return 0
-
-    lax.fori_loop(0, OWN, supports, 0)
+    copies[10].wait()
+    copies[11].wait()
     for c in range(3):
         for h in range(16):
             load_ref[c * 16 + h : c * 16 + h + 1, :] = vel[c : c + 1, h * 256 : h * 256 + 256]
     table = split2(load_ref[...])
 
-    def answer(b, _):
+    for b in range(OWN):
         out = dot_nn(table, sup_lo[b])
         out = out[0:48] + out[48:96]
         hot = sup_hi[b]
@@ -354,39 +403,30 @@
         rows.append(jnp.zeros((1, 128), F32))
         for c in range(4):
             wall_send[b, c : c + 1, :] = rows[c]
-        return 0
-
-    lax.fori_loop(0, OWN, answer, 0)
     wall_recv[own] = wall_send[own]
     to_owners(lambda o: wall_send.at[o], wall_recv.at[own], s_wall, r_wall)
 
     def elements(values):
         both = split2(values)
 
-        def gather(j, _):
+        for j in range(8):
             out = dot_nn(both, el_lo[j])
             out = out[0:80] + out[80:160]
             hot = el_hi[j]
             for c in range(3):
-                pick[pl.ds(c * 8 + j, 1), :] = jnp.sum(
+                pick[c * 8 + j : c * 8 + j + 1, :] = jnp.sum(
                     out[c * 24 : c * 24 + 24] * hot, axis=0, keepdims=True
                 )
-            return 0
-
-        lax.fori_loop(0, 8, gather, 0)
         picked = pick[...]
         spread[...] = exact_dot(gram, picked) * modulus[...]
-        ela[...] = jnp.zeros((160, 256), F32)
-
-        def scatter(j, _):
+        total = None
+        for j in range(8):
             hot = el_hi[j]
-            parts = [hot * spread[pl.ds(c * 8 + j, 1), :] for c in range(3)]
+            parts = [hot * spread[c * 8 + j : c * 8 + j + 1, :] for c in range(3)]
             parts.append(jnp.zeros((8, 512), F32))
-            ela[...] += dot_nt(split2(jnp.concatenate(parts, axis=0)), el_lo[j])
-            return 0
-
-        lax.fori_loop(0, 8, scatter, 0)
-        return ela[0:80] + ela[80:160], picked
+            part = dot_nt(split2(jnp.concatenate(parts, axis=0)), el_lo[j])
+            total = part if total is None else total + part
+        return total[0:80] + total[80:160], picked
 
     wait(edge_recv, r_edge)
     vec_r[...] = jnp.zeros((80, 256), F32)
@@ -399,8 +439,7 @@
             vec_x[c * 16 + h : c * 16 + h + 1, :] = row
         vec_r[c * 24 + 16 : c * 24 + 17, :] = edge_recv[c : c + 1, :] * has_before
     vec_w[...] = elements(vec_r[...])[0]
-    massc[:, 0:128] = mass[pl.ds(2 * f, 1), :]
-    massc[:, 128:256] = mass[pl.ds(2 * f + 1, 1), :]
+    massx[16:17, :] = edge_recv[3:4, :]
 
     wait(wall_recv.at[pl.ds(0, OWN - 1)], r_wall)
     wall = [None] * 4
@@ -448,9 +487,8 @@
     to_owners(lambda o: frc_send.at[o], frc_recv.at[own], s_frc, r_frc)
     wait(frc_recv.at[pl.ds(0, OWN - 1)], r_frc)
 
-    load_ref[...] = jnp.zeros((48, 256), F32)
-
-    def collect(b, _):
+    total = None
+    for b in range(OWN):
         force = frc_recv[b]
         parts = []
         for c in range(3):
@@ -458,81 +496,110 @@
             line = jnp.concatenate([line] * 4, axis=1)
             parts.append(sup_hi[b] * line)
         got = dot_nt(split2(jnp.concatenate(parts, axis=0)), sup_lo[b])
-        load_ref[...] += got[0:48] + got[48:96]
-        return 0
-
-    lax.fori_loop(0, OWN, collect, 0)
+        total = got if total is None else total + got
+    load_ref[...] = total[0:48] + total[48:96]
 
     row4w = iota((4, 256), 0)
-
-    def exchange(app, sums, with_mass):
+    place = lax.rem(f + 4, FX)
+    spot = lax.rem(place, 8)
+    high = jnp.where(place < 8, HIGH_RELAYS[0], HIGH_RELAYS[1])
+    low = high - 1
+    is_high = (f == HIGH_RELAYS[0]) | (f == HIGH_RELAYS[1])
+    is_low = (f == LOW_RELAYS[0]) | (f == LOW_RELAYS[1])
+    is_double = (f == HIGH_RELAYS[1]) | is_low
+    slot2 = jnp.where(f == HIGH_RELAYS[1], 16, jnp.where(f == LOW_RELAYS[0], 17, 18))
+    keep_after = jnp.where(is_high, has_after, 1.0)
+
+    def exchange(app, sums, scalars):
         for c in range(3):
             for h in range(17):
                 rs_send[app, h, c : c + 1, :] = sums[c * 24 + h : c * 24 + h + 1, :]
-        for h in range(17):
-            rs_send[app, h, 3:4, :] = jnp.zeros((1, 256), F32)
+        top, ghost = rs_send.at[app, 15], rs_send.at[app, 16]
+        send(ghost, rl_recv.at[app, 8 + spot], s_rl.at[app], r_rl.at[app], at_owner(before, high))
+        send(top, rl_recv.at[app, 8 + spot], s_rl.at[app], r_rl.at[app], at_owner(after, low))
+        for d in FAR_X:
+            j = lax.rem(f + d, FX)
+
+            @pl.when(j < 15)
+            def _():
+                send(rs_send.at[app, j], rs_recv.at[app, f], s_rs.at[app], r_rs.at[app], (j, y, z))
+
+        @pl.when(f != high)
+        def _():
+            send(top, rl_recv.at[app, spot], s_rl.at[app], r_rl.at[app], (high, y, z))
+
+        @pl.when(f != low)
+        def _():
+            send(ghost, rl_recv.at[app, spot], s_rl.at[app], r_rl.at[app], (low, y, z))
+
+        if scalars is not None:
+            to_owners(lambda o: sc_send.at[app], sc_recv.at[app, own], s_sc.at[app], r_sc.at[app])
         rs_recv[app, f] = rs_send[app, f]
 
-        def go(d, _):
-            j = lax.rem(f + d, FX)
-            send(rs_send.at[app, j], rs_recv.at[app, f], s_rs.at[app], r_rs.at[app], (j, y, z))
-            return 0
-
-        lax.fori_loop(1, FX, go, 0)
-        send(
-            rs_send.at[app, 16], gh_recv.at[app, f], s_gh.at[app], r_gh.at[app],
-            at_owner(before, FX - 1),
-        )
-        if with_mass is not None:
-            to_owners(lambda o: sc_send.at[app], sc_recv.at[app, own], s_sc.at[app], r_sc.at[app])
-        wait(rs_recv.at[app, pl.ds(0, FX - 1)], r_rs.at[app])
-        total = rs_recv[app, 0]
-        for n in range(1, FX):
-            total = total + rs_recv[app, n]
-        ag_send[app] = total
-
-        @pl.when(f == FX - 1)
-        def _():
-            wait(gh_recv.at[app], r_gh.at[app])
-            extra = gh_recv[app, 0]
+        @pl.when(f < 15)
+        def _():
+            wait(rs_recv.at[app, pl.ds(0, FX - 1)], r_rs.at[app])
+            total = rs_recv[app, 0]
             for n in range(1, FX):
-                extra = extra + gh_recv[app, n]
-            ag_send[app] = ag_send[app] + extra * has_after
-
-        if with_mass is not None:
+                total = total + rs_recv[app, n]
+            ag_send[app, 0] = total
+
+        @pl.when(is_high | is_low)
+        def _():
+            rl_recv[app, spot] = rs_send[app, jnp.where(is_high, 15, 16)]
+            wait(rl_recv.at[app, pl.ds(0, 15)], r_rl.at[app])
+            here, there = rl_recv[app, 0], rl_recv[app, 8]
+            for n in range(1, 8):
+                here = here + rl_recv[app, n]
+                there = there + rl_recv[app, 8 + n]
+            ag_send[app, 1] = here + keep_after * there
+
+        @pl.when(is_double)
+        def _():
+            ag_recv[app, slot2] = ag_send[app, 1]
+            for d in FAR_X:
+                send(
+                    ag_send.at[app, 1], ag_recv.at[app, slot2], s_ag2.at[app], r_ag.at[app],
+                    (lax.rem(f + d, FX), y, z),
+                )
+
+        @pl.when(f == 15)
+        def _():
+            ag_send[app, 0] = ag_send[app, 1]
+
+        if scalars is not None:
             wait(sc_recv.at[app, pl.ds(0, OWN - 1)], r_sc.at[app])
             part = sc_recv[app, 0]
             for n in range(1, OWN):
                 part = part + sc_recv[app, n]
-            mine = ag_send[app] + with_mass
-            ag_send[app] = jnp.where(row4w == 3, jnp.concatenate([part, part], axis=1), mine)
-        ag_recv[app, f] = ag_send[app]
-
-        def spread_out(d, _):
-            j = lax.rem(f + d, FX)
-            send(ag_send.at[app], ag_recv.at[app, f], s_ag.at[app], r_ag.at[app], (j, y, z))
-            return 0
-
-        lax.fori_loop(1, FX, spread_out, 0)
-
-        @pl.when(f == FX - 1)
-        def _():
-            def onward(j, _):
-                send(
-                    ag_send.at[app], ag_recv.at[app, 16], s_ag2.at[app], r_ag.at[app],
-                    at_owner(after, j),
-                )
-                return 0
-
-            lax.fori_loop(0, FX, onward, 0)
-
-        wait(ag_recv.at[app, pl.ds(0, FX)], r_ag.at[app])
+            ag_send[app, 0] = jnp.where(
+                row4w == 3, jnp.concatenate([part, part], axis=1), ag_send[app, 0]
+            )
+        for d in FAR_X:
+            send(
+                ag_send.at[app, 0], ag_recv.at[app, f], s_ag.at[app], r_ag.at[app],
+                (lax.rem(f + d, FX), y, z),
+            )
+        ag_recv[app, f] = ag_send[app, 0]
+
+        @pl.when(is_double)
+        def _():
+            wait(ag_recv.at[app, pl.ds(0, 17)], r_ag.at[app])
+
+        @pl.when(jnp.logical_not(is_double))
+        def _():
+            wait(ag_recv.at[app, pl.ds(0, 18)], r_ag.at[app])
 
     def gathered(app, target):
         for c in range(3):
-            for h in range(16):
+            for h in range(15):
                 target[c * 24 + h : c * 24 + h + 1, :] = ag_recv[app, h, c : c + 1, :]
-            target[c * 24 + 16 : c * 24 + 17, :] = ag_recv[app, 16, c : c + 1, :] * has_before
+            target[c * 24 + 15 : c * 24 + 16, :] = (
+                ag_recv[app, 15, c : c + 1, :] + ag_recv[app, 16, c : c + 1, :]
+            )
+            target[c * 24 + 16 : c * 24 + 17, :] = has_before * (
+                ag_recv[app, 17, c : c + 1, :] + ag_recv[app, 18, c : c + 1, :]
+            )
 
     kdisp = vec_w[...]
     pad8 = jnp.zeros((8, 256), F32)
@@ -553,7 +620,7 @@
             rc[c : c + 1, :] = vec_r[pl.ds(c * 24 + f, 1), :]
         rc[3:4, :] = jnp.zeros((1, 256), F32)
         chunk = rc[...]
-        weighted = massc[...] * chunk
+        weighted = massx[pl.ds(f, 1), :] * chunk
         mine = jnp.sum(chunk * chunk, keepdims=True)
         energy = jnp.sum(picked * spread[...], keepdims=True) + jnp.sum(
             weighted * chunk, keepdims=True
@@ -561,7 +628,7 @@
         scalars = jnp.where(lane == 0, mine, jnp.where(lane == 1, energy, 0.0))
         sc_send[app] = scalars
         sc_recv[app, own] = scalars
-        exchange(app, sums, weighted)
+        exchange(app, sums, scalars)
         gathered(app, vec_w)
         both = ag_recv[app, 0]
         for n in range(1, FX):
@@ -570,8 +637,10 @@
         delta = both[3:4, 1:2]
         beta = jnp.where(app == 1, 0.0, new / gamma)
         alpha = new / (delta - beta * new / alpha)
+        weights = massx[...]
+        weights = jnp.concatenate([weights] * 3 + [pad8], axis=0)
         p = vec_r[...] + beta * vec_p[...]
-        s = vec_w[...] + beta * vec_s[...]
+        s = vec_w[...] + weights * vec_r[...] + beta * vec_s[...]
         vec_p[...] = p
         vec_s[...] = s
         vec_r[...] = vec_r[...] - alpha * s
@@ -596,18 +665,29 @@
         for n, (src, dst, device) in enumerate(jobs):
             wait(src, s_halo.at[step, n])
     for app in range(APPS):
-        wait(rs_recv.at[app, pl.ds(0, FX - 1)], s_rs.at[app])
-        wait(rs_send.at[app, 16], s_gh.at[app])
+        wait(rs_recv.at[app, pl.ds(0, 14)], s_rs.at[app])
+        wait(rs_recv.at[app, pl.ds(0, 3)], s_rl.at[app])
         if app:
             wait(sc_recv.at[app, pl.ds(0, OWN - 1)], s_sc.at[app])
         wait(ag_recv.at[app, pl.ds(0, FX - 1)], s_ag.at[app])
 
-        @pl.when(f == FX - 1)
-        def _():
-            wait(ag_recv.at[app, pl.ds(0, FX)], s_ag2.at[app])
+        @pl.when(f == 15)
+        def _():
+            wait(rs_recv.at[app, 0], s_rs.at[app])
+
+        @pl.when(jnp.logical_not(is_high | is_low))
+        def _():
+            wait(rs_recv.at[app, 0], s_rl.at[app])
+
+        @pl.when(is_double)
+        def _():
+            wait(ag_recv.at[app, pl.ds(0, FX - 1)], s_ag2.at[app])
 
 
 SCRATCH = dict(
+    pop=(19, 4, 8, 256), relax=(4, 8, 256), vel=(3, 4096), count=((1, 16), I32),
+    cell=((16, 32), I32), node=((16, 16, 32), I32), weight=(16, 16, 32), disp=(3, 4096),
+    mass=(32, 128), connect=((8, 512), I32), modulus=(1, 512), basis=(24, 24),
     sup_send=(16, 8, 128), sup_recv=(16, 8, 128),
     wall_send=(16, 4, 128), wall_recv=(16, 4, 128),
     frc_send=(16, 4, 128), frc_recv=(16, 4, 128),
@@ -617,16 +697,16 @@
     ds=(2, 4, 1, 256), dr=(2, 4, 1, 256),
     zs=(2, 4, 8, 128), zr=(2, 4, 8, 128), zxr=(2, 2, 8, 128),
     zys=(2, 2, 4, 128), zyr=(2, 2, 4, 128),
-    rs_send=(APPS, 17, 4, 256), rs_recv=(APPS, 16, 4, 256), gh_recv=(APPS, 16, 4, 256),
+    rs_send=(APPS, 17, 4, 256), rs_recv=(APPS, 16, 4, 256), rl_recv=(APPS, 16, 4, 256),
     sc_send=(APPS, 1, 128), sc_recv=(APPS, 16, 1, 128),
-    ag_send=(APPS, 4, 256), ag_recv=(APPS, 17, 4, 256),
+    ag_send=(APPS, 2, 4, 256), ag_recv=(APPS, 19, 4, 256),
     post=(19, 4, 8, 256), field=(19, 4, 8, 256), rho_ref=(4, 8, 256), gain=(3, 4, 8, 256),
     cell_lo=((256, 512), BF16), cell_hi=(32, 512), live_ref=(8, 128), wallp=((192, 512), BF16),
-    sup_lo=((16, 256, 512), BF16), sup_hi=(16, 16, 512), lhs=(8, 128),
+    sup_lo=((16, 256, 512), BF16), sup_hi=(16, 16, 512),
     el_lo=((8, 256, 512), BF16), el_hi=(8, 24, 512),
-    pick=(24, 512), spread=(24, 512), ela=(160, 256),
+    pick=(24, 512), spread=(24, 512),
     vec_r=(80, 256), vec_p=(80, 256), vec_s=(80, 256), vec_w=(80, 256), vec_x=(48, 256),
-    massc=(1, 256), rc=(4, 256), load_ref=(48, 256),
+    massx=(24, 256), rc=(4, 256), load_ref=(48, 256),
 )
 
 
@@ -638,7 +718,7 @@
             shape, kind = shape
         shapes.append(pltpu.VMEM(shape, kind))
     dma = pltpu.SemaphoreType.DMA
-    shapes += [dma] * 8 + [dma((2, 13))] * 2 + [dma((APPS,))] * 9
+    shapes += [dma((INPUTS,))] + [dma] * 8 + [dma((2, 13))] * 2 + [dma((APPS,))] * 9
     return shapes
 
 
@@ -647,6 +727,7 @@
     disp_prev, node_mass, connect, modulus, strain_basis,
 ):
     vmem = pl.BlockSpec(memory_space=pltpu.VMEM)
+    hbm = pl.BlockSpec(memory_space=pl.ANY)
     return pl.pallas_call(
         kernel,
         out_shape=(
@@ -654,11 +735,11 @@
             jax.ShapeDtypeStruct(disp_prev.shape, F32),
             jax.ShapeDtypeStruct(disp_prev.shape, F32),
         ),
-        in_specs=[vmem] * 12,
+        in_specs=[hbm] * INPUTS,
         out_specs=(vmem, vmem, vmem),
         scratch_shapes=scratch_shapes(),
         compiler_params=pltpu.CompilerParams(
-            has_side_effects=True, vmem_limit_bytes=48 * 1024 * 1024
+            collective_id=0, has_side_effects=True, vmem_limit_bytes=48 * 1024 * 1024
         ),
         name="window",
     )(

time: 134 us -> 99.6 us (0.74)
  Pallas kernels: 122 us -> 87.5 us
    pallas_call x1, Pallas kernels: 122 us -> 87.5 us  [body(): pl.pallas_call(kernel, out_shape=(jax.ShapeDtypeStruct(populations.shape,...]
where the time goes in v2:
time: 99.6 us; the launch traced here: 99.1 us
  Pallas kernels  87.5 us (88%)
  local copies, waits for them, and re-layouts  10.9 us (11%)
    pallas_call x1, Pallas kernels, body(): pl.pallas_call(kernel, out_shape=(jax.ShapeDtypeStruct(populations.shape,...  87.5 us
    unnamed x27, local copies, waits for them, and re-layouts  10.9 us

profile of v2, /device:TPU:1, one launch (start us, length us, event | category | flops | bytes accessed | tf_op | source)
XLA Modules:
  0.0 99.1 jit_solution(2362168638894657581)
XLA Ops:
  0.6 0.0 copy-start.8
  0.6 0.0 copy-start.11
  0.7 0.7 copy-done.8
  1.3 0.0 copy-done.11
  1.3 0.0 copy-start
  1.3 1.1 %copy-done = f32[19,4,8,256]{3,2,1,0:T(8,128)S(1)} copy-done((f32[19,4,8,256]{3,2,1,0:T(8,128)S(1)}, f32[19,4,8,256]{3,2,1,0:T(8,128)}, u32[]{:S(2)}) %copy-start) | copy-done | bytes 622616
  2.4 0.0 copy-start.1
  2.4 0.9 copy-done.1
  3.3 0.0 copy-start.2
  3.3 0.9 copy-done.2
  4.2 0.0 copy-start.3
  4.2 0.8 copy-done.3
  5.1 0.0 copy-start.4
  5.1 0.8 copy-done.4
  5.9 0.0 copy-start.5
  5.9 0.8 copy-done.5
  6.7 0.7 copy-done.6
  7.4 0.7 copy-done.7
  8.1 0.7 copy-done.9
  8.8 0.7 copy-done.10
  9.5 87.5 %window.1 = (f32[19,4,8,256]{3,2,1,0:T(8,128)S(1)}, f32[3,4096]{1,0:T(4,128)S(1)}, f32[3,4096]{1,0:T(4,128)S(1)}) custom-call(f32[19,4,8,256]{3,2,1,0:T(8,128)S(1)} %copy-done, f32[4,8,256]{2,1,0:T(8,128)S(1)} %copy-done.5, f32[3,4096]{1,0:T(4,128)S(1)} %copy-done.3, s32[1,16]{1,0:T(1,128)S(1)} %bitcast.13, s32[16,32]{1,0:T(8,128)S(1)} %bitcast.11, ...), custom_call_target="tpu_custom_call" | custom-call | tf_op jit(solution)/shard_map/window/pallas_call | solution.py:731
  97.0 0.8 copy.18
  97.8 0.6 copy.19
  98.5 0.6 copy.20
  (4 shorter events, 0.0 us)
Async XLA Ops:
  0.6 0.7 copy-start.8
  0.6 0.7 copy-start.11
  1.3 1.1 %copy-start = (f32[19,4,8,256]{3,2,1,0:T(8,128)S(1)}, f32[19,4,8,256]{3,2,1,0:T(8,128)}, u32[]{:S(2)}) copy-start(f32[19,4,8,256]{3,2,1,0:T(8,128)} %pop_h.1) | copy-start | bytes 1867780
  2.4 0.9 copy-start.1
  3.3 0.9 copy-start.2
  4.2 0.8 copy-start.3
  5.1 0.8 copy-start.4
  5.9 0.8 copy-start.5
  6.7 0.7 copy-start.6
  7.4 0.7 copy-start.7
  8.1 0.7 copy-start.9
  8.8 0.7 copy-start.10

commit v3 on v2

--- a/solution.py
+++ b/solution.py
@@ -123,14 +123,14 @@
 def kernel(
     pop_h, relax_h, vel_h, count_h, cell_h, node_h, weight_h, disp_h, mass_h, connect_h,
     modulus_h, basis_h,
-    out_pop, out_sol, out_res,
+    out_pop_h, out_sol, out_res,
     pop, relax, vel, count, cell, node, weight, disp, mass, connect, modulus, basis,
     sup_send, sup_recv, wall_send, wall_recv, frc_send, frc_recv, edge_send, edge_recv,
     xs, xr, ys, yr, ds, dr, zs, zr, zxr, zys, zyr,
     rs_send, rs_recv, rl_recv, sc_send, sc_recv, ag_send, ag_recv,
     post, field, rho_ref, gain, cell_lo, cell_hi, live_ref, wallp,
     sup_lo, sup_hi, el_lo, el_hi, pick, spread, vec_r, vec_p, vec_s, vec_w, vec_x,
-    massx, rc, load_ref, s_in,
+    massx, rc, load_ref, out_pop, s_in, s_out,
     s_sup, r_sup, s_wall, r_wall, s_frc, r_frc, s_edge, r_edge, s_halo, r_halo,
     s_rs, r_rs, s_rl, r_rl, s_sc, r_sc, s_ag, r_ag, s_ag2,
 ):
@@ -462,6 +462,9 @@
     collide(field)
     jobs1 = stream(1, out_pop, wall_gain)
 
+    pop_copy = pltpu.make_async_copy(out_pop, out_pop_h, s_out)
+    pop_copy.start()
+
     rows = [[], [], [], []]
     for k in range(4):
         rho, mom = moments([out_pop[i, k] for i in range(19)])
@@ -657,6 +660,7 @@
             out_sol[c : c + 1, at] = vec_x[c * 16 + h : c * 16 + h + 1, :]
             out_res[c : c + 1, at] = vec_r[c * 24 + h : c * 24 + h + 1, :]
 
+    pop_copy.wait()
     wait(sup_recv.at[pl.ds(0, OWN - 1)], s_sup)
     wait(edge_send, s_edge)
     wait(wall_recv.at[pl.ds(0, OWN - 1)], s_wall)
@@ -706,7 +710,7 @@
     el_lo=((8, 256, 512), BF16), el_hi=(8, 24, 512),
     pick=(24, 512), spread=(24, 512),
     vec_r=(80, 256), vec_p=(80, 256), vec_s=(80, 256), vec_w=(80, 256), vec_x=(48, 256),
-    massx=(24, 256), rc=(4, 256), load_ref=(48, 256),
+    massx=(24, 256), rc=(4, 256), load_ref=(48, 256), out_pop=(19, 4, 8, 256),
 )
 
 
@@ -718,8 +722,25 @@
             shape, kind = shape
         shapes.append(pltpu.VMEM(shape, kind))
     dma = pltpu.SemaphoreType.DMA
-    shapes += [dma((INPUTS,))] + [dma] * 8 + [dma((2, 13))] * 2 + [dma((APPS,))] * 9
+    shapes += [dma((INPUTS,)), dma] + [dma] * 8 + [dma((2, 13))] * 2 + [dma((APPS,))] * 9
     return shapes
+
+
+def deliver(pop_h, sol_h, res_h, pop_out, sol_out, res_out, pop, sol, res, s_in, s_out):
+    jobs = [(pop_h.at[pl.ds(n, 4)], pop.at[pl.ds(n, 4)], pop_out.at[pl.ds(n, 4)]) for n in (0, 4, 8, 12)]
+    jobs.append((pop_h.at[pl.ds(16, 3)], pop.at[pl.ds(16, 3)], pop_out.at[pl.ds(16, 3)]))
+    jobs += [(sol_h, sol, sol_out), (res_h, res, res_out)]
+    copies = []
+    for n, (a, b, c) in enumerate(jobs):
+        copies.append(
+            (pltpu.make_async_copy(a, b, s_in.at[n]), pltpu.make_async_copy(b, c, s_out.at[n]))
+        )
+        copies[n][0].start()
+    for came, goes in copies:
+        came.wait()
+        goes.start()
+    for came, goes in copies:
+        goes.wait()
 
 
 def body(
@@ -728,18 +749,19 @@
 ):
     vmem = pl.BlockSpec(memory_space=pltpu.VMEM)
     hbm = pl.BlockSpec(memory_space=pl.ANY)
-    return pl.pallas_call(
+    shapes = (
+        jax.ShapeDtypeStruct(populations.shape, F32),
+        jax.ShapeDtypeStruct(disp_prev.shape, F32),
+        jax.ShapeDtypeStruct(disp_prev.shape, F32),
+    )
+    results = pl.pallas_call(
         kernel,
-        out_shape=(
-            jax.ShapeDtypeStruct(populations.shape, F32),
-            jax.ShapeDtypeStruct(disp_prev.shape, F32),
-            jax.ShapeDtypeStruct(disp_prev.shape, F32),
-        ),
+        out_shape=shapes,
         in_specs=[hbm] * INPUTS,
-        out_specs=(vmem, vmem, vmem),
+        out_specs=(hbm, vmem, vmem),
         scratch_shapes=scratch_shapes(),
         compiler_params=pltpu.CompilerParams(
-            collective_id=0, has_side_effects=True, vmem_limit_bytes=48 * 1024 * 1024
+            collective_id=0, has_side_effects=True, vmem_limit_bytes=62 * 1024 * 1024
         ),
         name="window",
     )(
@@ -756,6 +778,16 @@
         modulus.reshape(1, 512),
         strain_basis,
     )
+    return pl.pallas_call(
+        deliver,
+        out_shape=shapes,
+        in_specs=[hbm] * 3,
+        out_specs=(hbm, hbm, hbm),
+        scratch_shapes=[pltpu.VMEM(s.shape, F32) for s in shapes]
+        + [pltpu.SemaphoreType.DMA((7,))] * 2,
+        compiler_params=pltpu.CompilerParams(vmem_limit_bytes=62 * 1024 * 1024),
+        name="deliver",
+    )(*results)
 
 
 def solution(mesh):

time: 99.6 us -> 91.2 us (0.916)
  local copies, waits for them, and re-layouts: 10.9 us -> 0 us
  Pallas kernels: 87.5 us -> 90.4 us
    unnamed x27 -> x0, local copies, waits for them, and re-layouts: 10.9 us -> none
    pallas_call x1 -> x2, Pallas kernels: 87.5 us -> 90.4 us  [the longest x1 88.4 us: body(): pl.pallas_call(kernel, out_shape=shapes, in_specs=[hbm] * INPUTS, out_spe...]
where the time goes in v3:
time: 91.2 us; the launch traced here: 91 us
  Pallas kernels  90.4 us (99%)
    pallas_call x1, Pallas kernels, body(): pl.pallas_call(kernel, out_shape=shapes, in_specs=[hbm] * INPUTS, out_spe...  88.4 us
    pallas_call x1, Pallas kernels, body(): pl.pallas_call(deliver, out_shape=shapes, in_specs=[hbm] * 3, out_specs=(...  1.96 us

profile of v3, /device:TPU:1, one launch (start us, length us, event | category | flops | bytes accessed | tf_op | source)
XLA Modules:
  0.0 91.0 jit_solution(10495036437965068567)
XLA Ops:
  0.6 88.4 %window.1 = (f32[19,4,8,256]{3,2,1,0:T(8,128)}, f32[3,4096]{1,0:T(4,128)}, f32[3,4096]{1,0:T(4,128)}) custom-call(f32[19,4,8,256]{3,2,1,0:T(8,128)} %pop_h.1, f32[4,8,256]{2,1,0:T(8,128)} %relax_h.1, f32[3,4096]{1,0:T(4,128)} %vel_h.1, s32[1,16]{1,0:T(1,128)} %bitcast.13, s32[16,32]{1,0:T(8,128)} %bitcast.11, s32[16,16,32]{2,1,0:T(8,128)} %bitcast.7, ...), custom_call_target="tpu_custom_call" | custom-call | tf_op jit(solution)/shard_map/window/pallas_call | solution.py:757
  89.1 2.0 %deliver.1 = (f32[19,4,8,256]{3,2,1,0:T(8,128)}, f32[3,4096]{1,0:T(4,128)}, f32[3,4096]{1,0:T(4,128)}) custom-call(f32[19,4,8,256]{3,2,1,0:T(8,128)} %get-tuple-element.6.pop_h, f32[3,4096]{1,0:T(4,128)} %get-tuple-element.7.sol_h, f32[3,4096]{1,0:T(4,128)} %get-tuple-element.8.res_h), custom_call_target="tpu_custom_call" | custom-call | tf_op jit(solution)/shard_map/deliver/pallas_call | solution.py:781

commit v4 on v3

--- a/solution.py
+++ b/solution.py
@@ -47,6 +47,7 @@
 HIGH_RELAYS = (15, 7)
 LOW_RELAYS = (14, 6)
 INPUTS = 12
+NEAR = 10
 
 
 def split2(x):
@@ -113,7 +114,7 @@
                 for n in range(8):
                     tell(((first + n) % FX, there // SZ, lax.rem(there, SZ)))
 
-    pl.semaphore_wait(sem, 15 + 15 + 6 + 2)
+    return sem
 
 
 def wait(ref, sem):
@@ -153,7 +154,10 @@
         (vel_h, vel), (modulus_h, modulus),
     ]
     copies = [pltpu.make_async_copy(a, b, s_in.at[n]) for n, (a, b) in enumerate(inputs)]
-    for copy in copies:
+    for copy in copies[:2]:
+        copy.start()
+    barrier = greet(f, y, z, own)
+    for copy in copies[2:]:
         copy.start()
 
     lane = iota((1, 128), 1)
@@ -175,8 +179,8 @@
     for o in range(OWN):
         sup_send[o] = jnp.where(upper, packed(spread_n, o), packed(spread_w, o))
     sup_recv[own] = sup_send[own]
-    greet(f, y, z, own)
-    to_owners(lambda o: sup_send.at[o], sup_recv.at[own], s_sup, r_sup)
+    pl.semaphore_wait(barrier, 15 + 15 + 6 + 2)
+    to_owners(lambda o: sup_send.at[o], sup_recv.at[own], s_sup, r_sup.at[own])
 
     copies[2].wait()
     copies[3].wait()
@@ -200,6 +204,10 @@
         el_hi[j] = jnp.where(iota((24, 512), 0) == hi, 1.0, 0.0)
     base = basis[...]
     gram = exact_dot(base, base, ((0,), (0,)))
+    thrice = lax.rem(iota((24, 96), 1), 32) == iota((24, 96), 0)
+    gram = exact_dot(gram, thrice.astype(F32))
+    gram_top = gram.astype(BF16).astype(F32)
+    gram = jnp.where(iota((24, 96), 1) < 64, gram_top, gram - gram_top).astype(BF16)
 
     copies[6].wait()
     copies[7].wait()
@@ -283,7 +291,37 @@
         for k in range(4):
             for c in range(3):
                 gain[c, k] = wall_gain[c][k] * rho_ref[k] * (1.0 / 6.0)
-        for x in range(4):
+        xp, xm = lax.rem(f + 1, FX), lax.rem(f + FX - 1, FX)
+        yp, ym = lax.rem(y + 1, FY), lax.rem(y + FY - 1, FY)
+        zo = 1 - z
+        jobs = {
+            "x0": (xs.at[step, 0], xr.at[step, 0], (xp, y, z)),
+            "x1": (xs.at[step, 1], xr.at[step, 1], (xm, y, z)),
+            "y0": (ys.at[step, 0], yr.at[step, 0], (f, yp, z)),
+            "y1": (ys.at[step, 1], yr.at[step, 1], (f, ym, z)),
+            "d0": (ds.at[step, 0], dr.at[step, 0], (xp, yp, z)),
+            "d1": (ds.at[step, 1], dr.at[step, 1], (xm, ym, z)),
+            "d2": (ds.at[step, 2], dr.at[step, 2], (xp, ym, z)),
+            "d3": (ds.at[step, 3], dr.at[step, 3], (xm, yp, z)),
+            "zx0": (zs.at[step, 0], zxr.at[step, 0], (xp, y, zo)),
+            "zx1": (zs.at[step, 3], zxr.at[step, 1], (xm, y, zo)),
+            "zy0": (zys.at[step, 0], zyr.at[step, 0], (f, yp, zo)),
+            "zy1": (zys.at[step, 1], zyr.at[step, 1], (f, ym, zo)),
+            "z": (zs.at[step], zr.at[step], (f, y, zo)),
+        }
+        index = {name: n for n, name in enumerate(jobs)}
+
+        def go(*names):
+            for name in names:
+                src, dst, device = jobs[name]
+                n = index[name]
+                send(src, dst, s_halo.at[step, n], r_halo.at[step, n], device)
+
+        def came(*names):
+            for name in names:
+                wait(jobs[name][1], r_halo.at[step, index[name]])
+
+        for x in (0, 3, 1, 2):
             zpack = jnp.zeros((8, 128), F32)
             for i in range(19):
                 cx, cy, cz = VEL[i]
@@ -311,31 +349,16 @@
             zs[step, x] = zpack
             zys[step, 0, x : x + 1, :] = zpack[0:1, :]
             zys[step, 1, x : x + 1, :] = zpack[7:8, :]
-        xp, xm = lax.rem(f + 1, FX), lax.rem(f + FX - 1, FX)
-        yp, ym = lax.rem(y + 1, FY), lax.rem(y + FY - 1, FY)
-        zo = 1 - z
-        jobs = [
-            (ds.at[step, 0], dr.at[step, 0], (xp, yp, z)),
-            (ds.at[step, 1], dr.at[step, 1], (xm, ym, z)),
-            (ds.at[step, 2], dr.at[step, 2], (xp, ym, z)),
-            (ds.at[step, 3], dr.at[step, 3], (xm, yp, z)),
-            (zs.at[step, 0], zxr.at[step, 0], (xp, y, zo)),
-            (zs.at[step, 3], zxr.at[step, 1], (xm, y, zo)),
-            (zys.at[step, 0], zyr.at[step, 0], (f, yp, zo)),
-            (zys.at[step, 1], zyr.at[step, 1], (f, ym, zo)),
-            (zs.at[step], zr.at[step], (f, y, zo)),
-            (ys.at[step, 0], yr.at[step, 0], (f, yp, z)),
-            (ys.at[step, 1], yr.at[step, 1], (f, ym, z)),
-            (xs.at[step, 0], xr.at[step, 0], (xp, y, z)),
-            (xs.at[step, 1], xr.at[step, 1], (xm, y, z)),
-        ]
-        for n, (src, dst, device) in enumerate(jobs):
-            send(src, dst, s_halo.at[step, n], r_halo.at[step, n], device)
-        for n, (src, dst, device) in enumerate(jobs):
-            wait(dst, r_halo.at[step, n])
+            if x == 0:
+                go("zx0", "d0", "d2", "x0")
+            if x == 3:
+                go("zx1", "d1", "d3", "x1")
+        go("zy0", "zy1", "z", "y0", "y1")
+        came("x0", "x1")
         for side in range(2):
             for n, i in enumerate(X_POPS[side]):
                 target[i, 0 if side == 0 else 3] = xr[step, side, n]
+        came("y0", "y1")
         for side in range(2):
             r = 0 if side == 0 else 7
             for n, i in enumerate(Y_POPS[side]):
@@ -343,10 +366,12 @@
                 for x in range(4):
                     if 0 <= x - cx <= 3:
                         target[i, x, r : r + 1, :] = yr[step, side, n, x : x + 1, :]
+        came("d0", "d1", "d2", "d3")
         for n, i in enumerate(DIAGONAL):
             cx, cy, _ = VEL[i]
             r = 0 if cy > 0 else 7
             target[i, 0 if cx > 0 else 3, r : r + 1, :] = dr[step, n]
+        came("z", "zx0", "zx1", "zy0", "zy1")
         z11, z12, z13, z14, z15, z16, z17, z18 = [Z_POPS.index(i) for i in range(11, 19)]
         for x in range(4):
             zin = zr[step, x]
@@ -366,45 +391,57 @@
                     target[i, x, :, 128:256] = jnp.where(
                         lane8 == 127, col, target[i, x, :, 128:256]
                     )
-        return jobs
+        return list(jobs.values())
 
     copies[8].wait()
     copies[9].wait()
     collide(pop)
 
-    wait(sup_recv.at[pl.ds(0, OWN - 1)], r_sup)
-
-    for b in range(OWN):
-        for r in range(4):
-            n = sup_recv[b, r : r + 1, :].astype(I32)
-            w = sup_recv[b, r + 4 : r + 5, :]
-            sup_lo[b, :, r * 128 : r * 128 + 128] = jnp.where(
-                iota((256, 128), 0) == lax.rem(n, 256), 1.0, 0.0
-            ).astype(BF16)
-            sup_hi[b, :, r * 128 : r * 128 + 128] = jnp.where(
-                iota((16, 128), 0) == n // 256, w, 0.0
-            )
     copies[10].wait()
     copies[11].wait()
     for c in range(3):
         for h in range(16):
             load_ref[c * 16 + h : c * 16 + h + 1, :] = vel[c : c + 1, h * 256 : h * 256 + 256]
     table = split2(load_ref[...])
-
-    for b in range(OWN):
-        out = dot_nn(table, sup_lo[b])
-        out = out[0:48] + out[48:96]
-        hot = sup_hi[b]
-        rows = []
-        for c in range(3):
-            m = out[c * 16 : c * 16 + 16] * hot
-            m = m[:, 0:128] + m[:, 128:256] + m[:, 256:384] + m[:, 384:512]
-            rows.append(jnp.sum(m, axis=0, keepdims=True))
-        rows.append(jnp.zeros((1, 128), F32))
-        for c in range(4):
-            wall_send[b, c : c + 1, :] = rows[c]
-    wall_recv[own] = wall_send[own]
-    to_owners(lambda o: wall_send.at[o], wall_recv.at[own], s_wall, r_wall)
+    steps = [(0, 0)] + list(reversed(FAR_OWN))
+    batches = [list(enumerate(steps))[:NEAR], list(enumerate(steps))[NEAR:]]
+
+    def partner(step):
+        there = (f, lax.rem(y + step[0], FY), lax.rem(z + step[1], SZ))
+        return there, there[1] * SZ + there[2]
+
+    for batch in batches:
+        for n, step in batch:
+            if n:
+                o = partner(step)[1]
+                wait(sup_recv.at[o], r_sup.at[o])
+        for n, step in batch:
+            there, o = partner(step)
+            tile = sup_recv[o]
+            for r in range(4):
+                node_row = tile[r : r + 1].astype(I32)
+                sup_lo[n, :, r * 128 : r * 128 + 128] = jnp.where(
+                    iota((256, 128), 0) == lax.rem(node_row, 256), 1.0, 0.0
+                ).astype(BF16)
+                sup_hi[n, :, r * 128 : r * 128 + 128] = jnp.where(
+                    iota((16, 128), 0) == node_row // 256, tile[r + 4 : r + 5], 0.0
+                )
+        for n, step in batch:
+            there, o = partner(step)
+            out = dot_nn(table, sup_lo[n])
+            out = out[0:48] + out[48:96]
+            hot = sup_hi[n]
+            for c in range(3):
+                m = out[c * 16 : c * 16 + 16] * hot
+                m = m[:, 0:128] + m[:, 128:256] + m[:, 256:384] + m[:, 384:512]
+                wall_send[n, c : c + 1, :] = jnp.sum(m, axis=0, keepdims=True)
+            wall_send[n, 3:4, :] = jnp.zeros((1, 128), F32)
+        for n, step in reversed(batch):
+            there, o = partner(step)
+            if n:
+                send(wall_send.at[n], wall_recv.at[own], s_wall, r_wall, there)
+            else:
+                wall_recv[own] = wall_send[0]
 
     def elements(values):
         both = split2(values)
@@ -418,7 +455,10 @@
                     out[c * 24 : c * 24 + 24] * hot, axis=0, keepdims=True
                 )
         picked = pick[...]
-        spread[...] = exact_dot(gram, picked) * modulus[...]
+        wide = jnp.concatenate([picked, jnp.zeros((8, 512), F32)], axis=0)
+        top = wide.astype(BF16)
+        rest = (wide - top.astype(F32)).astype(BF16)
+        spread[...] = dot_nn(gram, jnp.concatenate([top, rest, top], axis=0)) * modulus[...]
         total = None
         for j in range(8):
             hot = el_hi[j]
@@ -426,7 +466,7 @@
             parts.append(jnp.zeros((8, 512), F32))
             part = dot_nt(split2(jnp.concatenate(parts, axis=0)), el_lo[j])
             total = part if total is None else total + part
-        return total[0:80] + total[80:160], picked
+        return total[0:80] + total[80:160]
 
     wait(edge_recv, r_edge)
     vec_r[...] = jnp.zeros((80, 256), F32)
@@ -438,7 +478,7 @@
             vec_r[c * 24 + h : c * 24 + h + 1, :] = row
             vec_x[c * 16 + h : c * 16 + h + 1, :] = row
         vec_r[c * 24 + 16 : c * 24 + 17, :] = edge_recv[c : c + 1, :] * has_before
-    vec_w[...] = elements(vec_r[...])[0]
+    vec_w[...] = elements(vec_r[...])
     massx[16:17, :] = edge_recv[3:4, :]
 
     wait(wall_recv.at[pl.ds(0, OWN - 1)], r_wall)
@@ -487,19 +527,23 @@
         for q in range(4):
             frc_send[g * 4 + q] = group_sum(jnp.where(group == q, force, 0.0))
     frc_recv[own] = frc_send[own]
-    to_owners(lambda o: frc_send.at[o], frc_recv.at[own], s_frc, r_frc)
-    wait(frc_recv.at[pl.ds(0, OWN - 1)], r_frc)
+    to_owners(lambda o: frc_send.at[o], frc_recv.at[own], s_frc, r_frc.at[own])
 
     total = None
-    for b in range(OWN):
-        force = frc_recv[b]
-        parts = []
-        for c in range(3):
-            line = force[c : c + 1, :]
-            line = jnp.concatenate([line] * 4, axis=1)
-            parts.append(sup_hi[b] * line)
-        got = dot_nt(split2(jnp.concatenate(parts, axis=0)), sup_lo[b])
-        total = got if total is None else total + got
+    for batch in batches:
+        for n, step in batch:
+            if n:
+                o = partner(step)[1]
+                wait(frc_recv.at[o], r_frc.at[o])
+        for n, step in batch:
+            force = frc_recv[partner(step)[1]]
+            parts = []
+            for c in range(3):
+                line = force[c : c + 1, :]
+                line = jnp.concatenate([line] * 4, axis=1)
+                parts.append(sup_hi[n] * line)
+            got = dot_nt(split2(jnp.concatenate(parts, axis=0)), sup_lo[n])
+            total = got if total is None else total + got
     load_ref[...] = total[0:48] + total[48:96]
 
     row4w = iota((4, 256), 0)
@@ -536,6 +580,7 @@
             send(ghost, rl_recv.at[app, spot], s_rl.at[app], r_rl.at[app], (low, y, z))
 
         if scalars is not None:
+            scalars()
             to_owners(lambda o: sc_send.at[app], sc_recv.at[app, own], s_sc.at[app], r_sc.at[app])
         rs_recv[app, f] = rs_send[app, f]
 
@@ -576,7 +621,7 @@
             for n in range(1, OWN):
                 part = part + sc_recv[app, n]
             ag_send[app, 0] = jnp.where(
-                row4w == 3, jnp.concatenate([part, part], axis=1), ag_send[app, 0]
+                row4w == 3, part, ag_send[app, 0]
             )
         for d in FAR_X:
             send(
@@ -618,40 +663,42 @@
 
     def iteration(app, carry):
         alpha, gamma = carry
-        sums, picked = elements(vec_r[...])
         for c in range(3):
             rc[c : c + 1, :] = vec_r[pl.ds(c * 24 + f, 1), :]
         rc[3:4, :] = jnp.zeros((1, 256), F32)
         chunk = rc[...]
-        weighted = massx[pl.ds(f, 1), :] * chunk
         mine = jnp.sum(chunk * chunk, keepdims=True)
-        energy = jnp.sum(picked * spread[...], keepdims=True) + jnp.sum(
-            weighted * chunk, keepdims=True
-        )
-        scalars = jnp.where(lane == 0, mine, jnp.where(lane == 1, energy, 0.0))
-        sc_send[app] = scalars
-        sc_recv[app, own] = scalars
-        exchange(app, sums, scalars)
+        held = jnp.sum(massx[pl.ds(f, 1), :] * chunk * chunk, keepdims=True)
+
+        def tell():
+            energy = held + jnp.sum(pick[...] * spread[...], keepdims=True)
+            scalars = jnp.where(iota((1, 256), 1) < 128, mine, energy)
+            sc_send[app] = scalars
+            sc_recv[app, own] = scalars
+
+        exchange(app, elements(vec_r[...]), tell)
         gathered(app, vec_w)
         both = ag_recv[app, 0]
         for n in range(1, FX):
             both = both + ag_recv[app, n]
-        new = both[3:4, 0:1]
-        delta = both[3:4, 1:2]
+        new = both[3:4, 0:128]
+        delta = both[3:4, 128:256]
         beta = jnp.where(app == 1, 0.0, new / gamma)
         alpha = new / (delta - beta * new / alpha)
         weights = massx[...]
         weights = jnp.concatenate([weights] * 3 + [pad8], axis=0)
-        p = vec_r[...] + beta * vec_p[...]
-        s = vec_w[...] + weights * vec_r[...] + beta * vec_s[...]
+        beta2 = jnp.concatenate([beta, beta], axis=1)
+        alpha2 = jnp.concatenate([alpha, alpha], axis=1)
+        p = vec_r[...] + beta2 * vec_p[...]
+        s = vec_w[...] + weights * vec_r[...] + beta2 * vec_s[...]
         vec_p[...] = p
         vec_s[...] = s
-        vec_r[...] = vec_r[...] - alpha * s
+        vec_r[...] = vec_r[...] - alpha2 * s
         for c in range(3):
-            vec_x[c * 16 : c * 16 + 16, :] += alpha * p[c * 24 : c * 24 + 16, :]
+            vec_x[c * 16 : c * 16 + 16, :] += alpha2 * p[c * 24 : c * 24 + 16, :]
         return alpha, new
 
-    one = jnp.ones((1, 1), F32)
+    one = jnp.ones((1, 128), F32)
     lax.fori_loop(1, APPS, iteration, (one, one))
 
     for c in range(3):
@@ -702,7 +749,7 @@
     zs=(2, 4, 8, 128), zr=(2, 4, 8, 128), zxr=(2, 2, 8, 128),
     zys=(2, 2, 4, 128), zyr=(2, 2, 4, 128),
     rs_send=(APPS, 17, 4, 256), rs_recv=(APPS, 16, 4, 256), rl_recv=(APPS, 16, 4, 256),
-    sc_send=(APPS, 1, 128), sc_recv=(APPS, 16, 1, 128),
+    sc_send=(APPS, 1, 256), sc_recv=(APPS, 16, 1, 256),
     ag_send=(APPS, 2, 4, 256), ag_recv=(APPS, 19, 4, 256),
     post=(19, 4, 8, 256), field=(19, 4, 8, 256), rho_ref=(4, 8, 256), gain=(3, 4, 8, 256),
     cell_lo=((256, 512), BF16), cell_hi=(32, 512), live_ref=(8, 128), wallp=((192, 512), BF16),
@@ -722,7 +769,9 @@
             shape, kind = shape
         shapes.append(pltpu.VMEM(shape, kind))
     dma = pltpu.SemaphoreType.DMA
-    shapes += [dma((INPUTS,)), dma] + [dma] * 8 + [dma((2, 13))] * 2 + [dma((APPS,))] * 9
+    shapes += [dma((INPUTS,)), dma]
+    shapes += [dma, dma((OWN,)), dma, dma, dma, dma((OWN,)), dma, dma]
+    shapes += [dma((2, 13))] * 2 + [dma((APPS,))] * 9
     return shapes
 
 

time: 91.2 us -> 89 us (0.976)
  Pallas kernels: 90.4 us -> 88.2 us
    pallas_call x1, Pallas kernels: 88.4 us -> 86.3 us  [body(): pl.pallas_call(kernel, out_shape=shapes, in_specs=[hbm] * INPUTS, out_spe...]
where the time goes in v4:
time: 89 us; the launch traced here: 88.9 us
  Pallas kernels  88.2 us (99%)
    pallas_call x1, Pallas kernels, body(): pl.pallas_call(kernel, out_shape=shapes, in_specs=[hbm] * INPUTS, out_spe...  86.3 us
    pallas_call x1, Pallas kernels, body(): pl.pallas_call(deliver, out_shape=shapes, in_specs=[hbm] * 3, out_specs=(...  1.96 us

profile of v4, /device:TPU:1, one launch (start us, length us, event | category | flops | bytes accessed | tf_op | source)
XLA Modules:
  0.0 88.9 jit_solution(3148228845792585137)
XLA Ops:
  0.6 86.3 %window.1 = (f32[19,4,8,256]{3,2,1,0:T(8,128)}, f32[3,4096]{1,0:T(4,128)}, f32[3,4096]{1,0:T(4,128)}) custom-call(f32[19,4,8,256]{3,2,1,0:T(8,128)} %pop_h.1, f32[4,8,256]{2,1,0:T(8,128)} %relax_h.1, f32[3,4096]{1,0:T(4,128)} %vel_h.1, s32[1,16]{1,0:T(1,128)} %bitcast.13, s32[16,32]{1,0:T(8,128)} %bitcast.11, s32[16,16,32]{2,1,0:T(8,128)} %bitcast.7, ...), custom_call_target="tpu_custom_call" | custom-call | tf_op jit(solution)/shard_map/window/pallas_call | solution.py:806
  86.9 2.0 %deliver.1 = (f32[19,4,8,256]{3,2,1,0:T(8,128)}, f32[3,4096]{1,0:T(4,128)}, f32[3,4096]{1,0:T(4,128)}) custom-call(f32[19,4,8,256]{3,2,1,0:T(8,128)} %get-tuple-element.6.pop_h, f32[3,4096]{1,0:T(4,128)} %get-tuple-element.7.sol_h, f32[3,4096]{1,0:T(4,128)} %get-tuple-element.8.res_h), custom_call_target="tpu_custom_call" | custom-call | tf_op jit(solution)/shard_map/deliver/pallas_call | solution.py:830

commit v5 on v4

--- a/solution.py
+++ b/solution.py
@@ -133,7 +133,7 @@
     sup_lo, sup_hi, el_lo, el_hi, pick, spread, vec_r, vec_p, vec_s, vec_w, vec_x,
     massx, rc, load_ref, out_pop, s_in, s_out,
     s_sup, r_sup, s_wall, r_wall, s_frc, r_frc, s_edge, r_edge, s_halo, r_halo,
-    s_rs, r_rs, s_rl, r_rl, s_sc, r_sc, s_ag, r_ag, s_ag2,
+    s_rs, r_rs, s_rl, r_rl, s_sc, r_sc, s_ag, r_ag,
 ):
     f = lax.axis_index("fx")
     y = lax.axis_index("fy")
@@ -528,6 +528,12 @@
             frc_send[g * 4 + q] = group_sum(jnp.where(group == q, force, 0.0))
     frc_recv[own] = frc_send[own]
     to_owners(lambda o: frc_send.at[o], frc_recv.at[own], s_frc, r_frc.at[own])
+    wait(sup_recv.at[pl.ds(0, OWN - 1)], s_sup)
+    wait(edge_send, s_edge)
+    wait(wall_recv.at[pl.ds(0, OWN - 1)], s_wall)
+    for step, jobs in enumerate((jobs0, jobs1)):
+        for n, (src, dst, device) in enumerate(jobs):
+            wait(src, s_halo.at[step, n])
 
     total = None
     for batch in batches:
@@ -554,7 +560,6 @@
     is_high = (f == HIGH_RELAYS[0]) | (f == HIGH_RELAYS[1])
     is_low = (f == LOW_RELAYS[0]) | (f == LOW_RELAYS[1])
     is_double = (f == HIGH_RELAYS[1]) | is_low
-    slot2 = jnp.where(f == HIGH_RELAYS[1], 16, jnp.where(f == LOW_RELAYS[0], 17, 18))
     keep_after = jnp.where(is_high, has_after, 1.0)
 
     def exchange(app, sums, scalars):
@@ -602,15 +607,6 @@
                 there = there + rl_recv[app, 8 + n]
             ag_send[app, 1] = here + keep_after * there
 
-        @pl.when(is_double)
-        def _():
-            ag_recv[app, slot2] = ag_send[app, 1]
-            for d in FAR_X:
-                send(
-                    ag_send.at[app, 1], ag_recv.at[app, slot2], s_ag2.at[app], r_ag.at[app],
-                    (lax.rem(f + d, FX), y, z),
-                )
-
         @pl.when(f == 15)
         def _():
             ag_send[app, 0] = ag_send[app, 1]
@@ -623,12 +619,37 @@
             ag_send[app, 0] = jnp.where(
                 row4w == 3, part, ag_send[app, 0]
             )
-        for d in FAR_X:
-            send(
-                ag_send.at[app, 0], ag_recv.at[app, f], s_ag.at[app], r_ag.at[app],
-                (lax.rem(f + d, FX), y, z),
-            )
-        ag_recv[app, f] = ag_send[app, 0]
+        @pl.when(is_double)
+        def _():
+            for d in FAR_X:
+                send(
+                    ag_send.at[app], ag_recv.at[app, pl.ds(2 * f, 2)], s_ag.at[app], r_ag.at[app],
+                    (lax.rem(f + d, FX), y, z),
+                )
+            ag_recv[app, 2 * f + 1] = ag_send[app, 1]
+
+        @pl.when(jnp.logical_not(is_double))
+        def _():
+            for d in FAR_X:
+                send(
+                    ag_send.at[app, 0], ag_recv.at[app, 2 * f], s_ag.at[app], r_ag.at[app],
+                    (lax.rem(f + d, FX), y, z),
+                )
+
+        ag_recv[app, 2 * f] = ag_send[app, 0]
+
+        wait(rs_recv.at[app, pl.ds(0, 14)], s_rs.at[app])
+        wait(rs_recv.at[app, pl.ds(0, 3)], s_rl.at[app])
+        if scalars is not None:
+            wait(sc_recv.at[app, pl.ds(0, OWN - 1)], s_sc.at[app])
+
+        @pl.when(f == 15)
+        def _():
+            wait(rs_recv.at[app, 0], s_rs.at[app])
+
+        @pl.when(jnp.logical_not(is_high | is_low))
+        def _():
+            wait(rs_recv.at[app, 0], s_rl.at[app])
 
         @pl.when(is_double)
         def _():
@@ -641,12 +662,14 @@
     def gathered(app, target):
         for c in range(3):
             for h in range(15):
-                target[c * 24 + h : c * 24 + h + 1, :] = ag_recv[app, h, c : c + 1, :]
+                target[c * 24 + h : c * 24 + h + 1, :] = ag_recv[app, 2 * h, c : c + 1, :]
             target[c * 24 + 15 : c * 24 + 16, :] = (
-                ag_recv[app, 15, c : c + 1, :] + ag_recv[app, 16, c : c + 1, :]
+                ag_recv[app, 2 * HIGH_RELAYS[0], c : c + 1, :]
+                + ag_recv[app, 2 * HIGH_RELAYS[1] + 1, c : c + 1, :]
             )
             target[c * 24 + 16 : c * 24 + 17, :] = has_before * (
-                ag_recv[app, 17, c : c + 1, :] + ag_recv[app, 18, c : c + 1, :]
+                ag_recv[app, 2 * LOW_RELAYS[0] + 1, c : c + 1, :]
+                + ag_recv[app, 2 * LOW_RELAYS[1] + 1, c : c + 1, :]
             )
 
     kdisp = vec_w[...]
@@ -657,6 +680,8 @@
     loads.append(pad8)
     exchange(0, jnp.concatenate(loads, axis=0) - kdisp, None)
     gathered(0, vec_r)
+    wait(frc_recv.at[pl.ds(0, OWN - 1)], s_frc)
+    pop_copy.wait()
     vec_p[...] = jnp.zeros((80, 256), F32)
     vec_s[...] = jnp.zeros((80, 256), F32)
     vec_w[...] = jnp.zeros((80, 256), F32)
@@ -680,7 +705,7 @@
         gathered(app, vec_w)
         both = ag_recv[app, 0]
         for n in range(1, FX):
-            both = both + ag_recv[app, n]
+            both = both + ag_recv[app, 2 * n]
         new = both[3:4, 0:128]
         delta = both[3:4, 128:256]
         beta = jnp.where(app == 1, 0.0, new / gamma)
@@ -707,32 +732,12 @@
             out_sol[c : c + 1, at] = vec_x[c * 16 + h : c * 16 + h + 1, :]
             out_res[c : c + 1, at] = vec_r[c * 24 + h : c * 24 + h + 1, :]
 
-    pop_copy.wait()
-    wait(sup_recv.at[pl.ds(0, OWN - 1)], s_sup)
-    wait(edge_send, s_edge)
-    wait(wall_recv.at[pl.ds(0, OWN - 1)], s_wall)
-    wait(frc_recv.at[pl.ds(0, OWN - 1)], s_frc)
-    for step, jobs in enumerate((jobs0, jobs1)):
-        for n, (src, dst, device) in enumerate(jobs):
-            wait(src, s_halo.at[step, n])
     for app in range(APPS):
-        wait(rs_recv.at[app, pl.ds(0, 14)], s_rs.at[app])
-        wait(rs_recv.at[app, pl.ds(0, 3)], s_rl.at[app])
-        if app:
-            wait(sc_recv.at[app, pl.ds(0, OWN - 1)], s_sc.at[app])
         wait(ag_recv.at[app, pl.ds(0, FX - 1)], s_ag.at[app])
 
-        @pl.when(f == 15)
-        def _():
-            wait(rs_recv.at[app, 0], s_rs.at[app])
-
-        @pl.when(jnp.logical_not(is_high | is_low))
-        def _():
-            wait(rs_recv.at[app, 0], s_rl.at[app])
-
         @pl.when(is_double)
         def _():
-            wait(ag_recv.at[app, pl.ds(0, FX - 1)], s_ag2.at[app])
+            wait(ag_recv.at[app, pl.ds(0, FX - 1)], s_ag.at[app])
 
 
 SCRATCH = dict(
@@ -750,7 +755,7 @@
     zys=(2, 2, 4, 128), zyr=(2, 2, 4, 128),
     rs_send=(APPS, 17, 4, 256), rs_recv=(APPS, 16, 4, 256), rl_recv=(APPS, 16, 4, 256),
     sc_send=(APPS, 1, 256), sc_recv=(APPS, 16, 1, 256),
-    ag_send=(APPS, 2, 4, 256), ag_recv=(APPS, 19, 4, 256),
+    ag_send=(APPS, 2, 4, 256), ag_recv=(APPS, 32, 4, 256),
     post=(19, 4, 8, 256), field=(19, 4, 8, 256), rho_ref=(4, 8, 256), gain=(3, 4, 8, 256),
     cell_lo=((256, 512), BF16), cell_hi=(32, 512), live_ref=(8, 128), wallp=((192, 512), BF16),
     sup_lo=((16, 256, 512), BF16), sup_hi=(16, 16, 512),
@@ -771,7 +776,7 @@
     dma = pltpu.SemaphoreType.DMA
     shapes += [dma((INPUTS,)), dma]
     shapes += [dma, dma((OWN,)), dma, dma, dma, dma((OWN,)), dma, dma]
-    shapes += [dma((2, 13))] * 2 + [dma((APPS,))] * 9
+    shapes += [dma((2, 13))] * 2 + [dma((APPS,))] * 8
     return shapes
 
 

time: 89 us -> 87.7 us (0.985)
  Pallas kernels: 88.2 us -> 86.9 us
    pallas_call x1, Pallas kernels: 86.3 us -> 85 us  [body(): pl.pallas_call(kernel, out_shape=shapes, in_specs=[hbm] * INPUTS, out_spe...]
where the time goes in v5:
time: 87.7 us; the launch traced here: 87.6 us
  Pallas kernels  86.9 us (99%)
    pallas_call x1, Pallas kernels, body(): pl.pallas_call(kernel, out_shape=shapes, in_specs=[hbm] * INPUTS, out_spe...  85 us
    pallas_call x1, Pallas kernels, body(): pl.pallas_call(deliver, out_shape=shapes, in_specs=[hbm] * 3, out_specs=(...  1.96 us

profile of v5, /device:TPU:1, one launch (start us, length us, event | category | flops | bytes accessed | tf_op | source)
XLA Modules:
  0.0 87.6 jit_solution(3933578272616844200)
XLA Ops:
  0.6 85.0 %window.1 = (f32[19,4,8,256]{3,2,1,0:T(8,128)}, f32[3,4096]{1,0:T(4,128)}, f32[3,4096]{1,0:T(4,128)}) custom-call(f32[19,4,8,256]{3,2,1,0:T(8,128)} %pop_h.1, f32[4,8,256]{2,1,0:T(8,128)} %relax_h.1, f32[3,4096]{1,0:T(4,128)} %vel_h.1, s32[1,16]{1,0:T(1,128)} %bitcast.13, s32[16,32]{1,0:T(8,128)} %bitcast.11, s32[16,16,32]{2,1,0:T(8,128)} %bitcast.7, ...), custom_call_target="tpu_custom_call" | custom-call | tf_op jit(solution)/shard_map/window/pallas_call | solution.py:811
  85.6 2.0 %deliver.1 = (f32[19,4,8,256]{3,2,1,0:T(8,128)}, f32[3,4096]{1,0:T(4,128)}, f32[3,4096]{1,0:T(4,128)}) custom-call(f32[19,4,8,256]{3,2,1,0:T(8,128)} %get-tuple-element.6.pop_h, f32[3,4096]{1,0:T(4,128)} %get-tuple-element.7.sol_h, f32[3,4096]{1,0:T(4,128)} %get-tuple-element.8.res_h), custom_call_target="tpu_custom_call" | custom-call | tf_op jit(solution)/shard_map/deliver/pallas_call | solution.py:835

commit v6 on v5

--- a/solution.py
+++ b/solution.py
@@ -100,20 +100,6 @@
         tell((lax.rem(f + d, FX), y, z))
     for dy, dz in FAR_OWN:
         tell((f, lax.rem(y + dy, FY), lax.rem(z + dz, SZ)))
-    for dx in (1, FX - 1):
-        tell((lax.rem(f + dx, FX), y, 1 - z))
-        for dy in (1, FY - 1):
-            tell((lax.rem(f + dx, FX), lax.rem(y + dy, FY), z))
-    for relays, step in ((HIGH_RELAYS, 1), (LOW_RELAYS, OWN - 1)):
-        there = lax.rem(own + step, OWN)
-
-        for relay, first in zip(relays, (12, 4)):
-
-            @pl.when(f == relay)
-            def _():
-                for n in range(8):
-                    tell(((first + n) % FX, there // SZ, lax.rem(there, SZ)))
-
     return sem
 
 
@@ -130,7 +116,7 @@
     xs, xr, ys, yr, ds, dr, zs, zr, zxr, zys, zyr,
     rs_send, rs_recv, rl_recv, sc_send, sc_recv, ag_send, ag_recv,
     post, field, rho_ref, gain, cell_lo, cell_hi, live_ref, wallp,
-    sup_lo, sup_hi, el_lo, el_hi, pick, spread, vec_r, vec_p, vec_s, vec_w, vec_x,
+    sup_lo, sup_hi, el_lo, el_hi, el_gh, pick, spread, vec_r, vec_p, vec_s, vec_w, vec_x,
     massx, rc, load_ref, out_pop, s_in, s_out,
     s_sup, r_sup, s_wall, r_wall, s_frc, r_frc, s_edge, r_edge, s_halo, r_halo,
     s_rs, r_rs, s_rl, r_rl, s_sc, r_sc, s_ag, r_ag,
@@ -179,17 +165,19 @@
     for o in range(OWN):
         sup_send[o] = jnp.where(upper, packed(spread_n, o), packed(spread_w, o))
     sup_recv[own] = sup_send[own]
-    pl.semaphore_wait(barrier, 15 + 15 + 6 + 2)
+    pl.semaphore_wait(barrier, 15 + 15)
     to_owners(lambda o: sup_send.at[o], sup_recv.at[own], s_sup, r_sup.at[own])
 
     copies[2].wait()
     copies[3].wait()
     for c in range(3):
         edge_send[c : c + 1, :] = disp[c : c + 1, 3840:4096]
-    massx[...] = jnp.zeros((24, 256), F32)
+    massx[...] = jnp.zeros((64, 256), F32)
     for h in range(16):
         massx[h : h + 1, 0:128] = mass[2 * h : 2 * h + 1, :]
         massx[h : h + 1, 128:256] = mass[2 * h + 1 : 2 * h + 2, :]
+    massx[16:32, :] = massx[0:16, :]
+    massx[32:48, :] = massx[0:16, :]
     edge_send[3:4, :] = massx[15:16, :]
     after, before = lax.rem(own + 1, OWN), lax.rem(own + OWN - 1, OWN)
     send(edge_send, edge_recv, s_edge, r_edge, at_owner(after))
@@ -199,9 +187,10 @@
     for j in range(8):
         n = connect[j : j + 1, :]
         lo = lax.rem(n, 256)
-        hi = jnp.where(n < 256, 16, n // 256 - 1)
+        hi = n // 256 - 1
         el_lo[j] = jnp.where(iota((256, 512), 0) == lo, 1.0, 0.0).astype(BF16)
-        el_hi[j] = jnp.where(iota((24, 512), 0) == hi, 1.0, 0.0)
+        el_hi[j] = jnp.where(iota((16, 512), 0) == hi, 1.0, 0.0)
+        el_gh[j : j + 1, :] = jnp.where(n < 256, 1.0, 0.0)
     base = basis[...]
     gram = exact_dot(base, base, ((0,), (0,)))
     thrice = lax.rem(iota((24, 96), 1), 32) == iota((24, 96), 0)
@@ -448,12 +437,11 @@
 
         for j in range(8):
             out = dot_nn(both, el_lo[j])
-            out = out[0:80] + out[80:160]
-            hot = el_hi[j]
+            out = out[0:64] + out[64:128]
+            hot, ghost = el_hi[j], el_gh[j : j + 1, :]
             for c in range(3):
-                pick[c * 8 + j : c * 8 + j + 1, :] = jnp.sum(
-                    out[c * 24 : c * 24 + 24] * hot, axis=0, keepdims=True
-                )
+                found = jnp.sum(out[c * 16 : c * 16 + 16] * hot, axis=0, keepdims=True)
+                pick[c * 8 + j : c * 8 + j + 1, :] = found + out[48 + c : 49 + c] * ghost
         picked = pick[...]
         wide = jnp.concatenate([picked, jnp.zeros((8, 512), F32)], axis=0)
         top = wide.astype(BF16)
@@ -461,25 +449,28 @@
         spread[...] = dot_nn(gram, jnp.concatenate([top, rest, top], axis=0)) * modulus[...]
         total = None
         for j in range(8):
-            hot = el_hi[j]
-            parts = [hot * spread[c * 8 + j : c * 8 + j + 1, :] for c in range(3)]
-            parts.append(jnp.zeros((8, 512), F32))
+            hot, ghost = el_hi[j], el_gh[j : j + 1, :]
+            rows = [spread[c * 8 + j : c * 8 + j + 1, :] for c in range(3)]
+            last = jnp.zeros((8, 512), F32)
+            for c in range(3):
+                last = jnp.where(iota((8, 512), 0) == c, rows[c] * ghost, last)
+            parts = [hot * row for row in rows] + [last, jnp.zeros((8, 512), F32)]
             part = dot_nt(split2(jnp.concatenate(parts, axis=0)), el_lo[j])
             total = part if total is None else total + part
-        return total[0:80] + total[80:160]
+        return total[0:64] + total[64:128]
 
     wait(edge_recv, r_edge)
-    vec_r[...] = jnp.zeros((80, 256), F32)
+    vec_r[...] = jnp.zeros((64, 256), F32)
     has_before = (own > 0).astype(F32)
     has_after = (own < OWN - 1).astype(F32)
     for c in range(3):
         for h in range(16):
             row = disp[c : c + 1, h * 256 : h * 256 + 256]
-            vec_r[c * 24 + h : c * 24 + h + 1, :] = row
+            vec_r[c * 16 + h : c * 16 + h + 1, :] = row
             vec_x[c * 16 + h : c * 16 + h + 1, :] = row
-        vec_r[c * 24 + 16 : c * 24 + 17, :] = edge_recv[c : c + 1, :] * has_before
+        vec_r[48 + c : 49 + c, :] = edge_recv[c : c + 1, :] * has_before
     vec_w[...] = elements(vec_r[...])
-    massx[16:17, :] = edge_recv[3:4, :]
+    massx[48:51, :] = jnp.broadcast_to(edge_recv[3:4, :], (3, 256))
 
     wait(wall_recv.at[pl.ds(0, OWN - 1)], r_wall)
     wall = [None] * 4
@@ -564,8 +555,9 @@
 
     def exchange(app, sums, scalars):
         for c in range(3):
-            for h in range(17):
-                rs_send[app, h, c : c + 1, :] = sums[c * 24 + h : c * 24 + h + 1, :]
+            for h in range(16):
+                rs_send[app, h, c : c + 1, :] = sums[c * 16 + h : c * 16 + h + 1, :]
+            rs_send[app, 16, c : c + 1, :] = sums[48 + c : 49 + c, :]
         top, ghost = rs_send.at[app, 15], rs_send.at[app, 16]
         send(ghost, rl_recv.at[app, 8 + spot], s_rl.at[app], r_rl.at[app], at_owner(before, high))
         send(top, rl_recv.at[app, 8 + spot], s_rl.at[app], r_rl.at[app], at_owner(after, low))
@@ -662,34 +654,30 @@
     def gathered(app, target):
         for c in range(3):
             for h in range(15):
-                target[c * 24 + h : c * 24 + h + 1, :] = ag_recv[app, 2 * h, c : c + 1, :]
-            target[c * 24 + 15 : c * 24 + 16, :] = (
+                target[c * 16 + h : c * 16 + h + 1, :] = ag_recv[app, 2 * h, c : c + 1, :]
+            target[c * 16 + 15 : c * 16 + 16, :] = (
                 ag_recv[app, 2 * HIGH_RELAYS[0], c : c + 1, :]
                 + ag_recv[app, 2 * HIGH_RELAYS[1] + 1, c : c + 1, :]
             )
-            target[c * 24 + 16 : c * 24 + 17, :] = has_before * (
+            target[48 + c : 49 + c, :] = has_before * (
                 ag_recv[app, 2 * LOW_RELAYS[0] + 1, c : c + 1, :]
                 + ag_recv[app, 2 * LOW_RELAYS[1] + 1, c : c + 1, :]
             )
 
     kdisp = vec_w[...]
-    pad8 = jnp.zeros((8, 256), F32)
-    loads = []
-    for c in range(3):
-        loads += [FORCE_SCALE * load_ref[c * 16 : c * 16 + 16, :], pad8]
-    loads.append(pad8)
-    exchange(0, jnp.concatenate(loads, axis=0) - kdisp, None)
+    loads = jnp.concatenate([FORCE_SCALE * load_ref[...], jnp.zeros((16, 256), F32)], axis=0)
+    exchange(0, loads - kdisp, None)
     gathered(0, vec_r)
     wait(frc_recv.at[pl.ds(0, OWN - 1)], s_frc)
     pop_copy.wait()
-    vec_p[...] = jnp.zeros((80, 256), F32)
-    vec_s[...] = jnp.zeros((80, 256), F32)
-    vec_w[...] = jnp.zeros((80, 256), F32)
+    vec_p[...] = jnp.zeros((64, 256), F32)
+    vec_s[...] = jnp.zeros((64, 256), F32)
+    vec_w[...] = jnp.zeros((64, 256), F32)
 
     def iteration(app, carry):
         alpha, gamma = carry
         for c in range(3):
-            rc[c : c + 1, :] = vec_r[pl.ds(c * 24 + f, 1), :]
+            rc[c : c + 1, :] = vec_r[pl.ds(c * 16 + f, 1), :]
         rc[3:4, :] = jnp.zeros((1, 256), F32)
         chunk = rc[...]
         mine = jnp.sum(chunk * chunk, keepdims=True)
@@ -710,17 +698,14 @@
         delta = both[3:4, 128:256]
         beta = jnp.where(app == 1, 0.0, new / gamma)
         alpha = new / (delta - beta * new / alpha)
-        weights = massx[...]
-        weights = jnp.concatenate([weights] * 3 + [pad8], axis=0)
         beta2 = jnp.concatenate([beta, beta], axis=1)
         alpha2 = jnp.concatenate([alpha, alpha], axis=1)
         p = vec_r[...] + beta2 * vec_p[...]
-        s = vec_w[...] + weights * vec_r[...] + beta2 * vec_s[...]
+        s = vec_w[...] + massx[...] * vec_r[...] + beta2 * vec_s[...]
         vec_p[...] = p
         vec_s[...] = s
         vec_r[...] = vec_r[...] - alpha2 * s
-        for c in range(3):
-            vec_x[c * 16 : c * 16 + 16, :] += alpha2 * p[c * 24 : c * 24 + 16, :]
+        vec_x[...] += alpha2 * p[0:48]
         return alpha, new
 
     one = jnp.ones((1, 128), F32)
@@ -730,7 +715,7 @@
         for h in range(16):
             at = slice(h * 256, h * 256 + 256)
             out_sol[c : c + 1, at] = vec_x[c * 16 + h : c * 16 + h + 1, :]
-            out_res[c : c + 1, at] = vec_r[c * 24 + h : c * 24 + h + 1, :]
+            out_res[c : c + 1, at] = vec_r[c * 16 + h : c * 16 + h + 1, :]
 
     for app in range(APPS):
         wait(ag_recv.at[app, pl.ds(0, FX - 1)], s_ag.at[app])
@@ -759,10 +744,10 @@
     post=(19, 4, 8, 256), field=(19, 4, 8, 256), rho_ref=(4, 8, 256), gain=(3, 4, 8, 256),
     cell_lo=((256, 512), BF16), cell_hi=(32, 512), live_ref=(8, 128), wallp=((192, 512), BF16),
     sup_lo=((16, 256, 512), BF16), sup_hi=(16, 16, 512),
-    el_lo=((8, 256, 512), BF16), el_hi=(8, 24, 512),
+    el_lo=((8, 256, 512), BF16), el_hi=(8, 16, 512), el_gh=(8, 512),
     pick=(24, 512), spread=(24, 512),
-    vec_r=(80, 256), vec_p=(80, 256), vec_s=(80, 256), vec_w=(80, 256), vec_x=(48, 256),
-    massx=(24, 256), rc=(4, 256), load_ref=(48, 256), out_pop=(19, 4, 8, 256),
+    vec_r=(64, 256), vec_p=(64, 256), vec_s=(64, 256), vec_w=(64, 256), vec_x=(48, 256),
+    massx=(64, 256), rc=(4, 256), load_ref=(48, 256), out_pop=(19, 4, 8, 256),
 )
 
 

time: 87.7 us -> 86.9 us (level)
  no operation moved by 1% of the time
where the time goes in v6:
time: 86.9 us; the launch traced here: 86.8 us
  Pallas kernels  86.1 us (99%)
    pallas_call x1, Pallas kernels, body(): pl.pallas_call(kernel, out_shape=shapes, in_specs=[hbm] * INPUTS, out_spe...  84.2 us
    pallas_call x1, Pallas kernels, body(): pl.pallas_call(deliver, out_shape=shapes, in_specs=[hbm] * 3, out_specs=(...  1.96 us

profile of v6, /device:TPU:1, one launch (start us, length us, event | category | flops | bytes accessed | tf_op | source)
XLA Modules:
  0.0 86.8 jit_solution(8024552122087092055)
XLA Ops:
  0.6 84.2 %window.1 = (f32[19,4,8,256]{3,2,1,0:T(8,128)}, f32[3,4096]{1,0:T(4,128)}, f32[3,4096]{1,0:T(4,128)}) custom-call(f32[19,4,8,256]{3,2,1,0:T(8,128)} %pop_h.1, f32[4,8,256]{2,1,0:T(8,128)} %relax_h.1, f32[3,4096]{1,0:T(4,128)} %vel_h.1, s32[1,16]{1,0:T(1,128)} %bitcast.13, s32[16,32]{1,0:T(8,128)} %bitcast.11, s32[16,16,32]{2,1,0:T(8,128)} %bitcast.7, ...), custom_call_target="tpu_custom_call" | custom-call | tf_op jit(solution)/shard_map/window/pallas_call | solution.py:796
  84.8 2.0 %deliver.1 = (f32[19,4,8,256]{3,2,1,0:T(8,128)}, f32[3,4096]{1,0:T(4,128)}, f32[3,4096]{1,0:T(4,128)}) custom-call(f32[19,4,8,256]{3,2,1,0:T(8,128)} %get-tuple-element.6.pop_h, f32[3,4096]{1,0:T(4,128)} %get-tuple-element.7.sol_h, f32[3,4096]{1,0:T(4,128)} %get-tuple-element.8.res_h), custom_call_target="tpu_custom_call" | custom-call | tf_op jit(solution)/shard_map/deliver/pallas_call | solution.py:820

commit v7 on v6

--- a/solution.py
+++ b/solution.py
@@ -554,6 +554,8 @@
     keep_after = jnp.where(is_high, has_after, 1.0)
 
     def exchange(app, sums, scalars):
+        if scalars is not None:
+            scalars()
         for c in range(3):
             for h in range(16):
                 rs_send[app, h, c : c + 1, :] = sums[c * 16 + h : c * 16 + h + 1, :]
@@ -577,7 +579,6 @@
             send(ghost, rl_recv.at[app, spot], s_rl.at[app], r_rl.at[app], (low, y, z))
 
         if scalars is not None:
-            scalars()
             to_owners(lambda o: sc_send.at[app], sc_recv.at[app, own], s_sc.at[app], r_sc.at[app])
         rs_recv[app, f] = rs_send[app, f]
 

time: 86.9 us -> 87.2 us (level)
  no operation moved by 1% of the time
where the time goes in v7:
time: 87.2 us; the launch traced here: 87.1 us
  Pallas kernels  86.4 us (99%)
    pallas_call x1, Pallas kernels, body(): pl.pallas_call(kernel, out_shape=shapes, in_specs=[hbm] * INPUTS, out_spe...  84.5 us
    pallas_call x1, Pallas kernels, body(): pl.pallas_call(deliver, out_shape=shapes, in_specs=[hbm] * 3, out_specs=(...  1.96 us

profile of v7, /device:TPU:1, one launch (start us, length us, event | category | flops | bytes accessed | tf_op | source)
XLA Modules:
  0.0 87.1 jit_solution(10013517463997416325)
XLA Ops:
  0.6 84.5 %window.1 = (f32[19,4,8,256]{3,2,1,0:T(8,128)}, f32[3,4096]{1,0:T(4,128)}, f32[3,4096]{1,0:T(4,128)}) custom-call(f32[19,4,8,256]{3,2,1,0:T(8,128)} %pop_h.1, f32[4,8,256]{2,1,0:T(8,128)} %relax_h.1, f32[3,4096]{1,0:T(4,128)} %vel_h.1, s32[1,16]{1,0:T(1,128)} %bitcast.13, s32[16,32]{1,0:T(8,128)} %bitcast.11, s32[16,16,32]{2,1,0:T(8,128)} %bitcast.7, ...), custom_call_target="tpu_custom_call" | custom-call | tf_op jit(solution)/shard_map/window/pallas_call | solution.py:797
  85.1 2.0 %deliver.1 = (f32[19,4,8,256]{3,2,1,0:T(8,128)}, f32[3,4096]{1,0:T(4,128)}, f32[3,4096]{1,0:T(4,128)}) custom-call(f32[19,4,8,256]{3,2,1,0:T(8,128)} %get-tuple-element.6.pop_h, f32[3,4096]{1,0:T(4,128)} %get-tuple-element.7.sol_h, f32[3,4096]{1,0:T(4,128)} %get-tuple-element.8.res_h), custom_call_target="tpu_custom_call" | custom-call | tf_op jit(solution)/shard_map/deliver/pallas_call | solution.py:821
